TPU v7x, 32 devices: a whole 2x2x4 slice. The times are simulated.
32 devices in a mesh: dp: 4 (over y, x), ctx: 4 (over z), tp: 2 (over core).
Axes of the slice: x: 2, y: 2, z: 4, core: 2. Of those that a mesh axis runs over, the one named last changes fastest.
Arguments:
- xbc: bfloat16 [2048, 12288], P(('dp', 'ctx'), 'tp'), parts along dimension 0, may hold values from -6 to 6
- gate_in: bfloat16 [2048, 8192], P(('dp', 'ctx'), 'tp'), parts along dimension 0, may hold values from -6 to 6
- dt_raw: float32 [128, 2048], P('tp', ('dp', 'ctx')), parts along dimension 1, may hold values from -2 to 13.2
- dt_bias: float32 [512], P(('dp', 'tp')), parts along dimension 0, may hold values from -13 to -3
- a_log: float32 [128], P('tp'), may hold values from -0.7 to 0
- conv_weight: float32 [4, 12288], P(None, 'tp'), may hold values from -3 to 3
- conv_bias: float32 [12288], P('tp'), may hold values from -3 to 3
- skip_weight: float32 [128], P('tp'), may hold values from 0.5 to 1.5
- norm_gain: float32 [8192], P('tp'), may hold values from 0.5 to 1.5
- queries: bfloat16 [2048, 8192], P(('dp', 'ctx'), 'tp'), parts along dimension 0, may hold values from -10 to 10
- keys: bfloat16 [2048, 1024], P(('dp', 'ctx'), 'tp'), parts along dimension 0, may hold values from -6 to 6
- values: bfloat16 [2048, 1024], P(('dp', 'ctx'), 'tp'), parts along dimension 0, may hold values from -6 to 6
Outputs:
- mamba_out: bfloat16 [2048, 8192], P(('dp', 'ctx'), 'tp'), parts along dimension 0
- attn_out: bfloat16 [2048, 8192], P(('dp', 'ctx'), 'tp'), parts along dimension 0
There are 4 independent parts, one for each index of `dp`. A program takes and returns all parts, laid end to end along the dimension named above; an argument that names none is the same for every part. Nothing has to cross between parts.
All inputs are finite; a program needn't handle non-finite values.
Results may differ from a plain program's by a relative error of at most 0.0047.
Values may be sent and summed in bfloat16 or wider, within the bound.
A program may use at most 64 MiB of HBM per device.

v0:
```python
import math

import jax
import jax.numpy as jnp
from jax import lax
from jax.sharding import PartitionSpec as P

SSM_HEAD_DIM = 64
SSM_STATE = 256
SPAN_LEN = 128
KEY_DIM = 128


eps = 1e-05
highest = lax.Precision.HIGHEST
key_block = 512
neg_large = -1e30


def shifted(value, axis, by):
    size = lax.axis_size(axis)
    pairs = [(i, i + by) for i in range(size) if 0 <= i + by < size]
    return lax.ppermute(value, axis, pairs)


def prefix_2(part, axis, combine, identity):
    place = lax.axis_index(axis)
    gathered = jax.tree.map(lambda a: lax.all_gather(a, axis), part)
    state = jax.tree.map(lambda a, e: jnp.zeros_like(a) + jnp.asarray(e, a.dtype), part, identity)

    def one(lap, state):
        return combine(
            state, jax.tree.map(lambda a: lax.dynamic_index_in_dim(a, lap, 0, False), gathered)
        )

    return lax.fori_loop(0, place, one, state)


def mamba_part(
    xbc, gate_in, dt_raw, dt_bias, a_log, conv_weight, conv_bias, skip_weight, norm_gain
):
    local_rows = xbc.shape[0]
    head_count = dt_raw.shape[0]
    head_cols = head_count * SSM_HEAD_DIM
    group_count = (xbc.shape[1] - head_cols) // (2 * SSM_STATE)
    per_group = head_count // group_count
    taps_count = conv_weight.shape[0]
    rim_rows = shifted(xbc[local_rows - (taps_count - 1) :], "ctx", 1)
    extended = jnp.concatenate([rim_rows, xbc], axis=0).astype(jnp.float32)
    running = jnp.zeros(xbc.shape, jnp.float32) + conv_bias[None, :]
    for offset in range(taps_count):
        running = running + conv_weight[offset][None, :] * extended[offset : offset + local_rows]
    conv_out = jax.nn.silu(running).astype(jnp.bfloat16)
    span_count = local_rows // SPAN_LEN
    group_width = group_count * SSM_STATE
    inputs = conv_out[:, :head_cols].reshape(span_count, SPAN_LEN, head_count, SSM_HEAD_DIM)
    b_groups = conv_out[:, head_cols : head_cols + group_width].reshape(
        span_count, SPAN_LEN, group_count, SSM_STATE
    )
    c_groups = conv_out[:, head_cols + group_width :].reshape(
        span_count, SPAN_LEN, group_count, SSM_STATE
    )
    dt_step = jax.nn.softplus(dt_raw + dt_bias[:, None])
    log_decay = -dt_step * jnp.exp(a_log)[:, None]
    dt_step = dt_step.reshape(head_count, span_count, SPAN_LEN).transpose(1, 0, 2)
    log_decay = log_decay.reshape(head_count, span_count, SPAN_LEN).transpose(1, 0, 2)
    cumulative = jnp.cumsum(log_decay, axis=2)
    causal = jnp.arange(SPAN_LEN)[:, None] >= jnp.arange(SPAN_LEN)[None, :]
    decay_gaps = cumulative[:, :, :, None] - cumulative[:, :, None, :]
    decay_matrix = jnp.where(causal, jnp.exp(jnp.where(causal, decay_gaps, 0.0)), 0.0)
    products = jnp.einsum("ctgn,csgn->cgts", c_groups, b_groups, preferred_element_type=jnp.float32)
    mixing = (
        products[:, :, None]
        * decay_matrix.reshape(span_count, group_count, per_group, SPAN_LEN, SPAN_LEN)
        * dt_step.reshape(span_count, group_count, per_group, 1, SPAN_LEN)
    ).astype(jnp.bfloat16)
    inputs_grouped = inputs.reshape(span_count, SPAN_LEN, group_count, per_group, SSM_HEAD_DIM)
    within_block = jnp.einsum(
        "cgrts,csgrp->ctgrp", mixing, inputs_grouped, preferred_element_type=jnp.float32
    )
    tail_weight = dt_step * jnp.exp(cumulative[:, :, -1:] - cumulative)
    weighted = (inputs.astype(jnp.float32) * tail_weight.transpose(0, 2, 1)[..., None]).astype(
        jnp.bfloat16
    )
    block_state = jnp.einsum(
        "csgn,csgrp->cgrpn",
        b_groups,
        weighted.reshape(span_count, SPAN_LEN, group_count, per_group, SSM_HEAD_DIM),
        preferred_element_type=jnp.float32,
    ).reshape(span_count, head_count, SSM_HEAD_DIM, SSM_STATE)
    span_total = jnp.exp(cumulative[:, :, -1])
    local_state = jnp.zeros((head_count, SSM_HEAD_DIM, SSM_STATE), jnp.float32)
    local_decay = jnp.ones((head_count,), jnp.float32)
    prefix_states = local_state
    prefix_decay = local_decay
    local_state = span_total[0][:, None, None] * local_state + block_state[0]
    local_decay = local_decay * span_total[0]

    def combine(earlier, later_part):
        return (
            earlier[0] * later_part[0],
            later_part[0][:, None, None] * earlier[1] + later_part[1],
        )

    prefix = prefix_2(
        (local_decay, local_state),
        "ctx",
        combine,
        (jnp.ones_like(local_decay), jnp.zeros_like(local_state)),
    )
    incoming = prefix[1]
    entry_states = jnp.stack([prefix_decay[:, None, None] * incoming + prefix_states], axis=0)
    from_state = jnp.einsum(
        "ctgn,cgrpn->ctgrp",
        c_groups.astype(jnp.float32),
        entry_states.reshape(span_count, group_count, per_group, SSM_HEAD_DIM, SSM_STATE),
        precision=highest,
    ).reshape(span_count, SPAN_LEN, head_count, SSM_HEAD_DIM)
    from_state = from_state * jnp.exp(cumulative).transpose(0, 2, 1)[..., None]
    outputs = (
        within_block.reshape(span_count, SPAN_LEN, head_count, SSM_HEAD_DIM)
        + from_state
        + skip_weight[None, None, :, None] * inputs.astype(jnp.float32)
    )
    mixer = outputs.reshape(local_rows, head_cols) * jax.nn.silu(gate_in.astype(jnp.float32))
    grouped = mixer.reshape(local_rows, group_count, -1)
    norm_scale = lax.rsqrt(jnp.mean(grouped * grouped, axis=-1, keepdims=True) + eps)
    return ((grouped * norm_scale).reshape(local_rows, -1) * norm_gain[None, :]).astype(
        jnp.bfloat16
    )


def attend(running, key_rows, value_rows, block_start, query_heads, query_pos):
    row_best, row_total, row_accum = running
    group_count = query_heads.shape[1]
    key_heads = key_rows.reshape(key_rows.shape[0], group_count, -1)
    value_heads = value_rows.reshape(value_rows.shape[0], group_count, -1)
    score_scale = 1.0 / math.sqrt(key_heads.shape[2])
    scores = (
        jnp.einsum("qgrd,kgd->grqk", query_heads, key_heads, preferred_element_type=jnp.float32)
        * score_scale
    )
    key_pos = block_start + jnp.arange(key_rows.shape[0], dtype=jnp.int32)
    allowed = key_pos[None, :] <= query_pos[:, None]
    block_best = jnp.max(jnp.where(allowed, scores, neg_large), axis=-1)
    newest = jnp.maximum(row_best, block_best)
    weights = jnp.where(allowed, jnp.exp(scores - newest[..., None]), 0.0)
    factor = jnp.exp(row_best - newest)
    row_total = row_total * factor + jnp.sum(weights, axis=-1)
    row_accum = row_accum * factor[..., None] + jnp.einsum(
        "grqk,kgd->grqd",
        weights.astype(jnp.bfloat16),
        value_heads,
        preferred_element_type=jnp.float32,
    )
    return (newest, row_total, row_accum)


def make_fold(query_heads, query_pos):

    def fold_keys(running, pieces, first_row):
        key_piece, value_piece = pieces
        piece_rows = key_piece.shape[0]
        block_count = piece_rows // key_block
        key_blocks = key_piece.reshape(block_count, key_block, key_piece.shape[1])
        value_blocks = value_piece.reshape(block_count, key_block, value_piece.shape[1])
        starts = first_row + key_block * jnp.arange(block_count, dtype=jnp.int32)

        def visit(carried, block_items):
            key_rows, value_rows, block_start = block_items
            updated = attend(carried, key_rows, value_rows, block_start, query_heads, query_pos)
            return (updated, None)

        result, unused = lax.scan(visit, running, (key_blocks, value_blocks, starts))
        return result

    return fold_keys


def shards(
    xbc,
    gate_in,
    dt_raw,
    dt_bias,
    a_log,
    conv_weight,
    conv_bias,
    skip_weight,
    norm_gain,
    queries,
    keys,
    values,
):
    mamba_out = mamba_part(
        xbc, gate_in, dt_raw, dt_bias, a_log, conv_weight, conv_bias, skip_weight, norm_gain
    )
    local_rows = queries.shape[0]
    group_count = keys.shape[1] // KEY_DIM
    repeat_count = queries.shape[1] // keys.shape[1]
    query_heads = queries.reshape(local_rows, group_count, repeat_count, KEY_DIM)
    query_pos = lax.axis_index("ctx") * local_rows + jnp.arange(local_rows, dtype=jnp.int32)
    initial = (
        jnp.full((group_count, repeat_count, local_rows), neg_large, jnp.float32),
        jnp.zeros((group_count, repeat_count, local_rows), jnp.float32),
        jnp.zeros((group_count, repeat_count, local_rows, KEY_DIM), jnp.float32),
    )
    fold_keys = make_fold(query_heads, query_pos)
    whole_keys, whole_values = (
        lax.all_gather(keys, "ctx", axis=0, tiled=True),
        lax.all_gather(values, "ctx", axis=0, tiled=True),
    )
    finished = fold_keys(initial, (whole_keys, whole_values), 0)
    top_score, row_total, row_accum = finished
    attn_out = (
        (row_accum / row_total[..., None])
        .transpose(2, 0, 1, 3)
        .reshape(local_rows, -1)
        .astype(jnp.bfloat16)
    )
    return (mamba_out, attn_out)


def solution(mesh):
    placed = (
        P(("dp", "ctx"), "tp"),
        P(("dp", "ctx"), "tp"),
        P("tp", ("dp", "ctx")),
        P(("dp", "tp")),
        P("tp"),
        P(None, "tp"),
        P("tp"),
        P("tp"),
        P("tp"),
        P(("dp", "ctx"), "tp"),
        P(("dp", "ctx"), "tp"),
        P(("dp", "ctx"), "tp"),
    )
    return jax.shard_map(
        shards,
        mesh=mesh,
        in_specs=placed,
        out_specs=(P(("dp", "ctx"), "tp"), P(("dp", "ctx"), "tp")),
        check_vma=False,
    )
```

profile of v0, /device:TPU:24, one launch (start us, length us, event | category | flops | bytes accessed | tf_op | source)
XLA Modules:
  0.0 361.5 jit_solution(10034287969927784596)
XLA Ops:
  7.2 0.0 all-gather.3.cloned.1.call-start
  7.2 0.9 slice.41
  8.1 1.3 collective-permute-start
  9.4 1.2 fusion.45
  10.6 0.7 exp.78
  11.3 0.9 multiply_bitcast_fusion
  12.2 0.3 reduce_window_sum.13
  12.4 0.1 slice.60
  12.5 0.1 copy.77
  12.6 0.1 fusion.39
  12.7 1.9 copy.50
  14.6 0.9 copy.49
  15.5 0.0 copy-start.7
  15.5 1.1 maximum_convert_fusion
  16.7 7.9 %multiply_convert_fusion.1 = bf16[128,6144]{0,1:T(8,128)(2,1)S(1)} fusion(f32[131,6144]{0,1:T(8,128)S(1)} %maximum_convert_fusion, f32[6144]{0:T(1024)S(1)} %bitcast.148, f32[6144]{0:T(1024)S(1)} %bitcast.149, f32[6144]{0:T(1024)S(1)} %bitcast.147, f32[6144]{0:T(1024)S(1)} %bitcast.146, f32[6144]{0:T(1024)S(1)} %copy-done.7), kind=kLoop, calls=%fused_computation.25 | loop fusion | flops 10223616 | bytes 14278656 | tf_op jit(solution)/shard_map/convert_element_type | solution.py:53
  24.6 0.1 slice.57
  24.7 1.0 copy-done.1
  25.7 0.7 fusion.34
  26.4 2.3 bitcast_add_fusion.1
  28.7 0.0 all-gather.3.cloned.1.call-update
  28.7 1.2 copy-done.4
  29.9 1.3 copy.56
  31.2 0.1 mul.247
  31.3 0.1 mul.248
  31.3 1.4 copy.78
  32.8 1.0 copy.57
  33.8 20.4 %all_gather.16 = bf16[512,512]{1,0:T(8,128)(2,1)} all-gather(bf16[128,512]{1,0:T(8,128)(2,1)S(1)} %copy-done.6), channel_id=1, replica_groups=mesh['dp'=4,'ctx'=4,'tp'=2] {'ctx'}, dimensions={0}, use_global_device_ids=true | all-gather | bytes 655360 | tf_op jit(solution)/shard_map/all_gather | solution.py:210
  54.2 2.0 copy.60
  56.3 33.4 %all_gather.15 = bf16[512,512]{0,1:T(8,128)(2,1)S(1)} all-gather(bf16[128,512]{0,1:T(8,128)(2,1)S(1)} %copy.57), channel_id=1, replica_groups=mesh['dp'=4,'ctx'=4,'tp'=2] {'ctx'}, dimensions={0}, use_global_device_ids=true | all-gather | bytes 655360 | tf_op jit(solution)/shard_map/all_gather | solution.py:209
  89.8 2.0 fusion
  91.9 0.0 copy-start.5
  91.9 1.8 fusion.3
  93.8 2.9 fusion.23
  96.7 2.3 copy.63
  98.9 25.4 %all-gather = f32[4,64,1]{1,2,0:T(1,128)S(1)} all-gather(f32[1,64,1]{1,2,0:T(1,128)S(1)} %exp.80), channel_id=2, replica_groups=mesh['dp'=4,'ctx'=4,'tp'=2] {'ctx'}, dimensions={0}, use_global_device_ids=true | all-gather | bytes 1280 | tf_op jit(solution)/shard_map/all_gather | solution.py:28
  124.4 0.3 fusion.46
  124.7 3.3 fusion.15
  128.0 198.6 %all-gather.3.cloned.1.call-done = f32[4,64,64,256]{3,2,1,0:T(8,128)} async-done(((f32[1,64,64,256]{3,2,1,0:T(8,128)}), f32[4,64,64,256]{3,2,1,0:T(8,128)}) %all-gather.3.cloned.1.call-update) | async-done | bytes 16777232 | tf_op jit(solution)/shard_map/all_gather | solution.py:28
  326.6 2.5 broadcast.138
  329.1 17.6 %while.3 = (s32[]{:T(128)}, f32[64,64,256]{2,1,0:T(8,128)}, s32[]{:T(128)}, f32[4,64]{1,0:T(4,128)S(1)}, f32[4,64,64,256]{3,2,1,0:T(8,128)}, /*index=5*/s32[]{:T(128)}, s32[]{:T(128)}, s32[]{:T(128)}) while((s32[]{:T(128)}, f32[64,64,256]{2,1,0:T(8,128)}, s32[]{:T(128)}, f32[4,64]{1,0:T(4,128)S(1)}, f32[4,64,64,256]{3,2,1,0:T(8,128)}, ...), condition=%wide.region_2.3_spmd, body=%wide.region_1.2_spmd.sunk | while | flops 2097157 | bytes 12583807 | solution.py:36
  329.1 5.9 %bitcast_add_fusion.5 = f32[64,64,256]{2,1,0:T(8,128)} fusion(f32[4,64,64,256]{3,2,1,0:T(8,128)} %get-tuple-element.155, s32[]{:T(128)S(6)} %select_n.60, f32[64,64,256]{2,1,0:T(8,128)} %get-tuple-element.144, f32[64]{0:T(128)S(1)} %dynamic-slice_bitcast_fusion.2), kind=kLoop, calls=%fused_computation.clone.1 | loop fusion | flops 2097152 | bytes 12583172 | tf_op jit(solution)/shard_map/while/body/add | solution.py:102
  334.9 5.9 %bitcast_add_fusion.5 = f32[64,64,256]{2,1,0:T(8,128)} fusion(f32[4,64,64,256]{3,2,1,0:T(8,128)} %get-tuple-element.155, s32[]{:T(128)S(6)} %select_n.60, f32[64,64,256]{2,1,0:T(8,128)} %get-tuple-element.144, f32[64]{0:T(128)S(1)} %dynamic-slice_bitcast_fusion.2), kind=kLoop, calls=%fused_computation.clone.1 | loop fusion | flops 2097152 | bytes 12583172 | tf_op jit(solution)/shard_map/while/body/add | solution.py:102
  340.8 5.9 %bitcast_add_fusion.5 = f32[64,64,256]{2,1,0:T(8,128)} fusion(f32[4,64,64,256]{3,2,1,0:T(8,128)} %get-tuple-element.155, s32[]{:T(128)S(6)} %select_n.60, f32[64,64,256]{2,1,0:T(8,128)} %get-tuple-element.144, f32[64]{0:T(128)S(1)} %dynamic-slice_bitcast_fusion.2), kind=kLoop, calls=%fused_computation.clone.1 | loop fusion | flops 2097152 | bytes 12583172 | tf_op jit(solution)/shard_map/while/body/add | solution.py:102
  346.7 4.4 %fusion.47 = f32[4,16,64,128]{3,2,1,0:T(8,128)S(1)} fusion(f32[4,16,64,256]{3,2,1,0:T(8,128)} %bitcast.130, bf16[128,4,256,1]{0,2,3,1:T(8,128)(2,1)S(1)} %bitcast.137), kind=kOutput, calls=%fused_computation.74 | convolution fusion | flops 1610612736 | bytes 6553600 | tf_op jit(solution)/shard_map/ctgn,cgrpn->ctgrp/dot_general | solution.py:113
  351.2 0.0 copy-start.8
  351.2 1.4 bitcast_reduce_fusion
  352.7 0.7 fusion.25
  353.4 1.3 copy.62
  (29 shorter events, 0.2 us)
Async XLA Ops:
  7.2 319.4 %all-gather.3.cloned.1.call-start = ((), (), s32[]{:S(2)}) async-start(), calls=%async_computation | async-start | bytes 20971520 | tf_op jit(solution)/shard_map/all_gather | solution.py:28
  8.1 6.5 %collective-permute-start = (bf16[3,6144]{1,0:T(4,128)(2,1)S(1)}, bf16[3,6144]{1,0:T(4,128)(2,1)S(1)}, u32[]{:S(2)}, u32[]{:S(2)}) collective-permute-start(bf16[3,6144]{1,0:T(4,128)(2,1)S(1)} %slice.41), channel_id=1, source_target_pairs={{0,2},{2,4},{4,6},{1,3},{3,5},{5,7},{8,10},{10,12},{12,14},{9,11},... | collective-permute-start | bytes 110600 | tf_op jit(solution)/shard_map/ppermute | solution.py:23
  15.5 1.2 copy-start.7
  24.7 1.0 copy-start.1
  28.7 1.2 copy-start.4
  28.7 2.5 copy-start.9
  28.7 5.1 %copy-start.6 = (bf16[128,512]{1,0:T(8,128)(2,1)S(1)}, bf16[128,512]{1,0:T(8,128)(2,1)}, u32[]{:S(2)}) copy-start(bf16[128,512]{1,0:T(8,128)(2,1)} %param.25) | copy-start | bytes 393220
  91.9 1.9 copy-start.5
  93.7 31.0 %copy-start.2 = (bf16[128,4096]{0,1:T(8,128)(2,1)S(1)}, bf16[128,4096]{0,1:T(8,128)(2,1)}, u32[]{:S(2)}) copy-start(bf16[128,4096]{0,1:T(8,128)(2,1)} %copy-done.1) | copy-start | bytes 3145732
  346.7 4.5 %copy-start = (bf16[128,4096]{0,1:T(8,128)(2,1)S(1)}, bf16[128,4096]{0,1:T(8,128)(2,1)}, u32[]{:S(2)}) copy-start(bf16[128,4096]{0,1:T(8,128)(2,1)} %copy.56) | copy-start | bytes 3145732
  346.7 4.5 %copy-start.3 = (f32[4,16,64,128]{3,2,1,0:T(8,128)S(1)}, f32[4,16,64,128]{3,2,1,0:T(8,128)}, u32[]{:S(2)}) copy-start(f32[4,16,64,128]{3,2,1,0:T(8,128)} %fusion.15) | copy-start | bytes 6291460
  351.2 1.5 copy-start.8
Sparse Core Ops, SparseCore 0:
  28.8 297.7 all-gather.2
where the time goes:
time: 362 us
  waiting for transfers between devices  199 us (55%)
  blocking collectives  79.3 us (22%)
  other arithmetic  34.3 us (9%)
  local copies, waits for them, and re-layouts  20 us (6%)
  between operations  14.3 us (4%)
  matrix products  13.7 us (4%)
    all_gather x1, waiting for transfers between devices, prefix_2(): gathered = jax.tree.map(lambda a: lax.all_gather(a, axis), part)  199 us
    all_gather x1, blocking collectives, shards(): lax.all_gather(keys, 'ctx', axis=0, tiled=True)  33.4 us
    all_gather x1, blocking collectives, prefix_2(): gathered = jax.tree.map(lambda a: lax.all_gather(a, axis), part)  25.4 us
    all_gather x1, blocking collectives, shards(): lax.all_gather(values, 'ctx', axis=0, tiled=True)  20.4 us
    add x3, other arithmetic, combine(): later_part[0][:, None, None] * earlier[1] + later_part[1]  17.6 us
    unnamed x27, local copies, waits for them, and re-layouts  11.5 us
    convert_element_type x1, other arithmetic, mamba_part(): conv_out = jax.nn.silu(running).astype(jnp.bfloat16)  7.87 us
  transfers between devices with their start and end apart: 2, of which 1 were waited for; matrix products, arithmetic and copies ran while one was open for 7% of the time, Pallas kernels for 0%

commit v1 on v0

v1 whole, which is shorter than its diff:
```python
import functools
import math

import jax
import jax.numpy as jnp
from jax import lax
from jax.experimental import pallas as pl
from jax.experimental.pallas import tpu as pltpu
from jax.sharding import PartitionSpec as P

P_DIM = 64
N_STATE = 256
KEY_DIM = 128
CHUNK = 256
RIM = 16
EPS = 1e-05
NEG = -1e30
F32 = jnp.float32
BF16 = jnp.bfloat16


def dot(a, b):
    return jnp.dot(a, b, preferred_element_type=F32)


def dot_nt(a, b):
    return lax.dot_general(a, b, (((1,), (1,)), ((), ())), preferred_element_type=F32)


def silu(v):
    return v / (1.0 + jnp.exp(-v))


def log1p_unit(e):
    z = e / (2.0 + e)
    z2 = z * z
    acc = jnp.full_like(z, 1.0 / 17.0)
    for k in (15, 13, 11, 9, 7, 5, 3, 1):
        acc = acc * z2 + 1.0 / k
    return 2.0 * z * acc


def kernel(
    n,
    xbc,
    gate,
    dt_raw,
    dt_bias,
    a_log,
    conv_w,
    conv_b,
    skip,
    gain,
    queries,
    keys,
    values,
    mamba_out,
    attn_out,
    rim,
    xc,
    kbuf,
    vbuf,
    dt_row,
    cum_row,
    ecum_x,
    spread,
    s_own,
    h_in,
    h_out,
    y_acc,
    rim_send,
    rim_recv,
    k_send,
    k_recv,
    v_send,
    v_recv,
    h_send,
    h_recv,
):
    me = lax.axis_index("ctx")
    rows = xbc.shape[0]
    heads = dt_raw.shape[0]
    head_cols = heads * P_DIM
    groups = (xbc.shape[1] - head_cols) // (2 * N_STATE)
    per_group = heads // groups
    gcols = per_group * P_DIM
    per_chunks = gcols // CHUNK
    chunks = groups * per_chunks
    taps = conv_w.shape[0]
    kv_heads = keys.shape[1] // KEY_DIM
    repeat = queries.shape[1] // keys.shape[1]
    has_next = me < n - 1
    has_prev = me > 0
    right = me + 1

    def remote(src, dst, send, recv):
        return pltpu.make_async_remote_copy(
            src_ref=src,
            dst_ref=dst,
            send_sem=send,
            recv_sem=recv,
            device_id={"ctx": right},
            device_id_type=pl.DeviceIdType.MESH,
        )

    barrier = pltpu.get_barrier_semaphore()

    @pl.when(has_prev)
    def _():
        pl.semaphore_signal(
            barrier, inc=1, device_id={"ctx": me - 1}, device_id_type=pl.DeviceIdType.MESH
        )

    @pl.when(has_next)
    def _():
        pl.semaphore_wait(barrier, 1)

    def rim_copy():
        return remote(xbc.at[pl.ds(rows - RIM, RIM), :], rim, rim_send, rim_recv)

    def own_kv():
        return (
            remote(keys, kbuf.at[me], k_send.at[me], k_recv.at[me]),
            remote(values, vbuf.at[me], v_send.at[me], v_recv.at[me]),
        )

    def kv_copy(block):
        return (
            remote(kbuf.at[block], kbuf.at[block], k_send.at[block], k_recv.at[block]),
            remote(vbuf.at[block], vbuf.at[block], v_send.at[block], v_recv.at[block]),
        )

    def h_copy(c):
        return remote(h_out.at[c], h_in.at[c], h_send.at[c], h_recv.at[c])

    @pl.when(has_next)
    def _():
        rim_copy().start()
        for copy in own_kv():
            copy.start()

    kbuf[me] = keys[...]
    vbuf[me] = values[...]

    def clear(j, carry):
        @pl.when(j > me)
        def _():
            kbuf[j] = jnp.zeros(keys.shape, BF16)
            vbuf[j] = jnp.zeros(values.shape, BF16)

        return carry

    lax.fori_loop(0, n, clear, 0)

    def column(ref):
        return jnp.transpose(jnp.broadcast_to(ref[...], (rows, heads)))

    pre = dt_raw[...] + column(dt_bias)
    dt = jnp.maximum(pre, 0.0) + log1p_unit(jnp.exp(-jnp.abs(pre)))
    cum = -dt * jnp.exp(column(a_log))
    lane = lax.broadcasted_iota(jnp.int32, (heads, rows), 1)
    step = 1
    while step < rows:
        cum = cum + jnp.where(lane >= step, pltpu.roll(cum, step, 1), 0.0)
        step *= 2
    dt_row[...] = dt
    cum_row[...] = cum
    spread_row = lax.broadcasted_iota(jnp.int32, (3 * per_group, gcols), 0)
    spread_col = lax.broadcasted_iota(jnp.int32, (3 * per_group, gcols), 1)
    hit = lax.rem(spread_row, per_group) == spread_col // P_DIM
    spread[...] = jnp.where(hit, 1.0, 0.0).astype(BF16)

    def expand(v):
        hi = v.astype(BF16).astype(F32)
        rest = v - hi
        mid = rest.astype(BF16).astype(F32)
        low = rest - mid
        parts = jnp.transpose(jnp.concatenate([hi, mid, low], axis=0))
        return dot(parts.astype(BF16), spread[...])

    @pl.when(has_prev)
    def _():
        rim_copy().wait_recv()

    @pl.when(me == 0)
    def _():
        rim[...] = jnp.zeros(rim.shape, BF16)

    def conv_tile(start, width):
        cols = pl.ds(pl.multiple_of(start, 256), width)
        ext = jnp.concatenate([rim[:, cols].astype(F32), xbc[:, cols].astype(F32)], axis=0)
        acc = jnp.broadcast_to(conv_b[:, cols], (rows, width))
        for tap in range(taps):
            by = taps - 1 - tap
            moved = ext if by == 0 else pltpu.roll(ext, by, 0)
            acc = acc + conv_w[tap : tap + 1, cols] * moved[RIM:]
        out = silu(acc)
        xc[:, cols] = out.astype(BF16)
        return out

    def group_rows(g):
        return pl.ds(pl.multiple_of(g * per_group, per_group), per_group)

    def first(g, carry):
        b_part = conv_tile(head_cols + g * N_STATE, N_STATE)
        b_turned = jnp.transpose(b_part).astype(BF16)
        cum_g = cum_row[group_rows(g), :]
        dt_g = dt_row[group_rows(g), :]
        last = jnp.broadcast_to(cum_g[:, rows - 1 :], cum_g.shape)
        tail = expand(dt_g * jnp.exp(last - cum_g))
        for i in range(per_chunks):
            c = g * per_chunks + i
            x_part = conv_tile(c * CHUNK, CHUNK).astype(BF16).astype(F32)
            weighted = (x_part * tail[:, i * CHUNK : (i + 1) * CHUNK]).astype(BF16)
            own = dot(b_turned, weighted)
            s_own[c] = own

            @pl.when(me == 0)
            def _():
                h_out[c] = own.astype(BF16)
                h_copy(c).start()

        ecum_x[:, pl.ds(pl.multiple_of(g * gcols, gcols), gcols)] = expand(jnp.exp(cum_g))
        conv_tile(head_cols + (groups + g) * N_STATE, N_STATE)
        return carry

    lax.fori_loop(0, groups, first, 0)

    def within(g):
        b_part = xc[:, pl.ds(pl.multiple_of(head_cols + g * N_STATE, N_STATE), N_STATE)]
        c_part = xc[:, pl.ds(pl.multiple_of(head_cols + (groups + g) * N_STATE, N_STATE), N_STATE)]
        products = dot_nt(c_part, b_part)
        cum_g = cum_row[group_rows(g), :]
        dt_g = dt_row[group_rows(g), :]
        cum_t = jnp.transpose(cum_g)
        t_pos = lax.broadcasted_iota(jnp.int32, (rows, rows), 0)
        s_pos = lax.broadcasted_iota(jnp.int32, (rows, rows), 1)
        causal = s_pos <= t_pos
        low_half = lax.broadcasted_iota(jnp.int32, (rows, 2 * P_DIM), 1) < P_DIM
        for pair in range(per_group // 2):
            mixes = []
            for j in (2 * pair, 2 * pair + 1):
                gap = cum_t[:, j : j + 1] - cum_g[j : j + 1, :]
                decay = jnp.exp(jnp.where(causal, gap, NEG))
                mixes.append((products * decay * dt_g[j : j + 1, :]).astype(BF16))
            cols = pl.ds(pl.multiple_of(g * gcols + pair * 2 * P_DIM, 2 * P_DIM), 2 * P_DIM)
            x_pair = xc[:, cols].astype(F32)
            x_two = jnp.concatenate(
                [jnp.where(low_half, x_pair, 0.0), jnp.where(low_half, 0.0, x_pair)], axis=0
            ).astype(BF16)
            scale = jnp.where(
                low_half, skip[g * per_group + 2 * pair], skip[g * per_group + 2 * pair + 1]
            )
            y_acc[:, cols] = dot(jnp.concatenate(mixes, axis=1), x_two) + scale * x_pair

    pieces = kv_heads * 2
    piece_heads = repeat // 2
    log2_scale = 1.4426950408889634 / math.sqrt(KEY_DIM)

    def attend(piece):
        kv_cols = pl.ds(pl.multiple_of((piece // 2) * KEY_DIM, KEY_DIM), KEY_DIM)
        k_all = jnp.concatenate([kbuf[j, :, kv_cols] for j in range(n)], axis=0)
        v_all = jnp.concatenate([vbuf[j, :, kv_cols] for j in range(n)], axis=0)
        q_pos = me * rows + lax.broadcasted_iota(jnp.int32, (rows, n * rows), 0)
        k_pos = lax.broadcasted_iota(jnp.int32, (rows, n * rows), 1)
        allowed = k_pos <= q_pos
        for j in range(piece_heads):
            start = (piece * piece_heads + j) * KEY_DIM
            cols = pl.ds(pl.multiple_of(start, KEY_DIM), KEY_DIM)
            scores = jnp.where(allowed, dot_nt(queries[:, cols], k_all), NEG)
            top = jnp.max(scores, axis=1, keepdims=True)
            probs = jnp.exp2((scores - top) * log2_scale)
            total = jnp.sum(probs, axis=1, keepdims=True)
            attn_out[:, cols] = (dot(probs.astype(BF16), v_all) / total).astype(BF16)

    def relay(s):
        block = me - 1 - s

        @pl.when(block >= 0)
        def _():
            for copy in kv_copy(block):
                copy.wait_recv()

            @pl.when(has_next)
            def _():
                for copy in kv_copy(block):
                    copy.start()

    def finish(g):
        cols = pl.ds(pl.multiple_of(g * gcols, gcols), gcols)
        v = y_acc[:, cols] * silu(gate[:, cols].astype(F32))
        scale = lax.rsqrt(jnp.mean(v * v, axis=1, keepdims=True) + EPS)
        mamba_out[:, cols] = (v * scale * gain[:, cols]).astype(BF16)

    def chain(c, carry):
        g = c // per_chunks
        cols = pl.ds(pl.multiple_of(c * CHUNK, CHUNK), CHUNK)

        @pl.when(c < n - 1)
        def _():
            relay(c)

        @pl.when(has_prev)
        def _():
            h_copy(c).wait_recv()

            @pl.when(has_next)
            def _():
                total = ecum_x[rows - 1 : rows, cols]
                h_out[c] = (total * h_in[c].astype(F32) + s_own[c]).astype(BF16)
                h_copy(c).start()

        @pl.when(c < groups)
        def _():
            within(c)

        @pl.when(has_prev)
        def _():
            c_cols = pl.ds(
                pl.multiple_of(head_cols + (groups + g) * N_STATE, N_STATE), N_STATE
            )
            y_acc[:, cols] += ecum_x[:, cols] * dot(xc[:, c_cols], h_in[c])

        @pl.when(lax.rem(c, per_chunks) == per_chunks - 1)
        def _():
            finish(g)

        piece = c - lead

        @pl.when((piece >= 0) & (piece < pieces))
        def _():
            attend(piece)

        return carry

    lead = max(n - 1, groups)
    lax.fori_loop(0, chunks, chain, 0)
    for s in range(chunks, n - 1):
        relay(s)

    def rest(piece, carry):
        attend(piece)
        return carry

    if chunks - lead < pieces:
        lax.fori_loop(max(chunks - lead, 0), pieces, rest, 0)

    @pl.when(has_next)
    def _():
        rim_copy().wait_send()
        for copy in own_kv():
            copy.wait_send()

        def sent(c, carry):
            h_copy(c).wait_send()
            return carry

        lax.fori_loop(0, chunks, sent, 0)

        def sent_kv(block, carry):
            @pl.when(block < me)
            def _():
                for copy in kv_copy(block):
                    copy.wait_send()

            return carry

        lax.fori_loop(0, n, sent_kv, 0)


def shards(
    n,
    xbc,
    gate_in,
    dt_raw,
    dt_bias,
    a_log,
    conv_weight,
    conv_bias,
    skip_weight,
    norm_gain,
    queries,
    keys,
    values,
):
    rows = xbc.shape[0]
    heads = dt_raw.shape[0]
    head_cols = heads * P_DIM
    groups = (xbc.shape[1] - head_cols) // (2 * N_STATE)
    per_group = heads // groups
    chunks = head_cols // CHUNK
    vmem = pl.BlockSpec(memory_space=pltpu.VMEM)
    smem = pl.BlockSpec(memory_space=pltpu.SMEM)
    dma = pltpu.SemaphoreType.DMA
    return pl.pallas_call(
        functools.partial(kernel, n),
        out_shape=(
            jax.ShapeDtypeStruct((rows, head_cols), BF16),
            jax.ShapeDtypeStruct(queries.shape, BF16),
        ),
        in_specs=[vmem] * 7 + [smem] + [vmem] * 4,
        out_specs=(vmem, vmem),
        scratch_shapes=[
            pltpu.VMEM((RIM, xbc.shape[1]), BF16),
            pltpu.VMEM(xbc.shape, BF16),
            pltpu.VMEM((n,) + keys.shape, BF16),
            pltpu.VMEM((n,) + values.shape, BF16),
            pltpu.VMEM(dt_raw.shape, F32),
            pltpu.VMEM(dt_raw.shape, F32),
            pltpu.VMEM((rows, head_cols), F32),
            pltpu.VMEM((3 * per_group, per_group * P_DIM), BF16),
            pltpu.VMEM((chunks, N_STATE, CHUNK), F32),
            pltpu.VMEM((chunks, N_STATE, CHUNK), BF16),
            pltpu.VMEM((chunks, N_STATE, CHUNK), BF16),
            pltpu.VMEM((rows, head_cols), F32),
            dma,
            dma,
            dma((n,)),
            dma((n,)),
            dma((n,)),
            dma((n,)),
            dma((chunks,)),
            dma((chunks,)),
        ],
        compiler_params=pltpu.CompilerParams(
            collective_id=0, has_side_effects=True, vmem_limit_bytes=48 * 1024 * 1024
        ),
        name="mixers",
    )(
        xbc,
        gate_in,
        dt_raw,
        dt_bias.reshape(1, -1),
        a_log.reshape(1, -1),
        conv_weight,
        conv_bias.reshape(1, -1),
        skip_weight,
        norm_gain.reshape(1, -1),
        queries,
        keys,
        values,
    )


def solution(mesh):
    placed = (
        P(("dp", "ctx"), "tp"),
        P(("dp", "ctx"), "tp"),
        P("tp", ("dp", "ctx")),
        P(("dp", "tp")),
        P("tp"),
        P(None, "tp"),
        P("tp"),
        P("tp"),
        P("tp"),
        P(("dp", "ctx"), "tp"),
        P(("dp", "ctx"), "tp"),
        P(("dp", "ctx"), "tp"),
    )
    return jax.shard_map(
        functools.partial(shards, mesh.shape["ctx"]),
        mesh=mesh,
        in_specs=placed,
        out_specs=(P(("dp", "ctx"), "tp"), P(("dp", "ctx"), "tp")),
        check_vma=False,
    )
```

time: 362 us -> 86.8 us (0.24)
  waiting for transfers between devices: 199 us -> 0 us
  blocking collectives: 79.3 us -> 0 us
  Pallas kernels: 0 us -> 73 us
  other arithmetic: 34.3 us -> 0 us
  matrix products: 13.7 us -> 0 us
  between operations: 14.3 us -> 0.66 us
  local copies, waits for them, and re-layouts: 20 us -> 12.7 us
    all_gather x1 -> x0, waiting for transfers between devices: 199 us -> none  [prefix_2(): gathered = jax.tree.map(lambda a: lax.all_gather(a, axis), part)]
    all_gather x3 -> x0, blocking collectives: 79.3 us -> none  [the longest x1 33.4 us: shards(): lax.all_gather(keys, 'ctx', axis=0, tiled=True)]
    pallas_call x0 -> x1, Pallas kernels: none -> 73 us  [shards(): pl.pallas_call(functools.partial(kernel, n), out_shape=(jax.ShapeDtypeStr...]
    add x6 -> x0, other arithmetic: 19.9 us -> none  [the longest x3 17.6 us: combine(): later_part[0][:, None, None] * earlier[1] + later_part[1]]
    dot_general x6 -> x0, matrix products: 13.7 us -> none  [the longest x1 4.44 us: mamba_part(): jnp.einsum('ctgn,cgrpn->ctgrp', c_groups.astype(jnp.float32), entry_state...]
    convert_element_type x3 -> x0, other arithmetic: 9.72 us -> none  [the longest x1 7.87 us: mamba_part(): conv_out = jax.nn.silu(running).astype(jnp.bfloat16)]
    unnamed x27 -> x26, local copies, waits for them, and re-layouts: 11.5 us -> 12.7 us
  transfers between devices with their start and end apart: 2 -> 0, of which waited for: 1 -> 0; matrix products, arithmetic and copies ran while one was open for 7% -> 0% of each run, Pallas kernels for 0% -> 0%
where the time goes in v1:
time: 86.8 us; the launch traced here: 86.3 us
  Pallas kernels  73 us (84%)
  local copies, waits for them, and re-layouts  12.7 us (15%)
    pallas_call x1, Pallas kernels, shards(): pl.pallas_call(functools.partial(kernel, n), out_shape=(jax.ShapeDtypeStr...  73 us
    unnamed x26, local copies, waits for them, and re-layouts  12.7 us

profile of v1, /device:TPU:24, one launch (start us, length us, event | category | flops | bytes accessed | tf_op | source)
XLA Modules:
  0.0 86.3 jit_solution(9400181536547026214)
XLA Ops:
  0.6 0.0 copy-start
  0.6 1.4 %copy-done = bf16[128,6144]{1,0:T(8,128)(2,1)S(1)} copy-done((bf16[128,6144]{1,0:T(8,128)(2,1)S(1)}, bf16[128,6144]{1,0:T(8,128)(2,1)}, u32[]{:S(2)}) %copy-start) | copy-done | bytes 1572888
  2.0 0.0 copy-start.1
  2.0 1.2 %copy-done.1 = bf16[128,4096]{1,0:T(8,128)(2,1)S(1)} copy-done((bf16[128,4096]{1,0:T(8,128)(2,1)S(1)}, bf16[128,4096]{1,0:T(8,128)(2,1)}, u32[]{:S(2)}) %copy-start.1) | copy-done | bytes 1048600
  3.3 0.0 copy-start.2
  3.3 1.2 %copy-done.2 = bf16[128,4096]{1,0:T(8,128)(2,1)S(1)} copy-done((bf16[128,4096]{1,0:T(8,128)(2,1)S(1)}, bf16[128,4096]{1,0:T(8,128)(2,1)}, u32[]{:S(2)}) %copy-start.2) | copy-done | bytes 1048600
  4.5 0.0 copy-start.3
  4.5 0.9 %copy-done.3 = bf16[128,512]{1,0:T(8,128)(2,1)S(1)} copy-done((bf16[128,512]{1,0:T(8,128)(2,1)S(1)}, bf16[128,512]{1,0:T(8,128)(2,1)}, u32[]{:S(2)}) %copy-start.3) | copy-done | bytes 131096
  5.4 0.0 copy-start.4
  5.4 0.9 %copy-done.4 = bf16[128,512]{1,0:T(8,128)(2,1)S(1)} copy-done((bf16[128,512]{1,0:T(8,128)(2,1)S(1)}, bf16[128,512]{1,0:T(8,128)(2,1)}, u32[]{:S(2)}) %copy-start.4) | copy-done | bytes 131096
  6.3 0.0 copy-start.5
  6.3 0.9 %copy-done.5 = f32[4,6144]{1,0:T(4,128)S(1)} copy-done((f32[4,6144]{1,0:T(4,128)S(1)}, f32[4,6144]{1,0:T(4,128)}, u32[]{:S(2)}) %copy-start.5) | copy-done | bytes 98328
  7.2 0.0 copy-start.6
  7.2 0.8 copy-done.6
  8.0 0.0 copy-start.7
  8.0 0.7 copy-done.7
  8.7 0.0 copy-start.8
  8.7 0.7 copy-done.8
  9.4 0.0 copy-start.9
  9.4 0.7 copy-done.9
  10.1 0.0 copy-start.10
  10.1 0.7 copy-done.10
  10.7 0.0 copy-start.11
  10.7 0.7 copy-done.11
  11.4 73.0 %mixers.1 = (bf16[128,4096]{1,0:T(8,128)(2,1)S(1)}, bf16[128,4096]{1,0:T(8,128)(2,1)S(1)}) custom-call(bf16[128,6144]{1,0:T(8,128)(2,1)S(1)} %copy-done, bf16[128,4096]{1,0:T(8,128)(2,1)S(1)} %copy-done.1, f32[64,128]{1,0:T(8,128)S(1)} %copy-done.6, f32[1,64]{1,0:T(1,128)S(1)} %bitcast.6, f32[1,64]{1,0:T(1,128)S(1)} %bitcast.7, f32[4,6144]{1,0:T(4,128)S(1)} %copy-done.5, ...), custom_call_target="tpu_custom_call" | custom-call | tf_op jit(solution)/shard_map/mixers/pallas_call | solution.py:395
  84.4 1.0 %copy.16 = bf16[128,4096]{1,0:T(8,128)(2,1)} copy(bf16[128,4096]{1,0:T(8,128)(2,1)S(1)} %get-tuple-element.4) | data formatting | bytes 2097152
  85.3 1.0 %copy.17 = bf16[128,4096]{1,0:T(8,128)(2,1)} copy(bf16[128,4096]{1,0:T(8,128)(2,1)S(1)} %get-tuple-element.5) | data formatting | bytes 2097152
Async XLA Ops:
  0.6 1.4 %copy-start = (bf16[128,6144]{1,0:T(8,128)(2,1)S(1)}, bf16[128,6144]{1,0:T(8,128)(2,1)}, u32[]{:S(2)}) copy-start(bf16[128,6144]{1,0:T(8,128)(2,1)} %xbc.1) | copy-start | bytes 4718596
  2.0 1.2 %copy-start.1 = (bf16[128,4096]{1,0:T(8,128)(2,1)S(1)}, bf16[128,4096]{1,0:T(8,128)(2,1)}, u32[]{:S(2)}) copy-start(bf16[128,4096]{1,0:T(8,128)(2,1)} %gate.1) | copy-start | bytes 3145732
  3.3 1.2 %copy-start.2 = (bf16[128,4096]{1,0:T(8,128)(2,1)S(1)}, bf16[128,4096]{1,0:T(8,128)(2,1)}, u32[]{:S(2)}) copy-start(bf16[128,4096]{1,0:T(8,128)(2,1)} %queries.1) | copy-start | bytes 3145732
  4.5 0.9 %copy-start.3 = (bf16[128,512]{1,0:T(8,128)(2,1)S(1)}, bf16[128,512]{1,0:T(8,128)(2,1)}, u32[]{:S(2)}) copy-start(bf16[128,512]{1,0:T(8,128)(2,1)} %keys.1) | copy-start | bytes 393220
  5.4 0.9 %copy-start.4 = (bf16[128,512]{1,0:T(8,128)(2,1)S(1)}, bf16[128,512]{1,0:T(8,128)(2,1)}, u32[]{:S(2)}) copy-start(bf16[128,512]{1,0:T(8,128)(2,1)} %values.1) | copy-start | bytes 393220
  6.3 0.9 %copy-start.5 = (f32[4,6144]{1,0:T(4,128)S(1)}, f32[4,6144]{1,0:T(4,128)}, u32[]{:S(2)}) copy-start(f32[4,6144]{1,0:T(4,128)} %conv_w.1) | copy-start | bytes 294916
  7.2 0.8 copy-start.6
  8.0 0.7 copy-start.7
  8.7 0.7 copy-start.8
  9.4 0.7 copy-start.9
  10.1 0.7 copy-start.10
  10.7 0.7 copy-start.11

commit v2 on v1

--- a/solution.py
+++ b/solution.py
@@ -13,6 +13,7 @@
 KEY_DIM = 128
 CHUNK = 256
 RIM = 16
+RIM_WIDTH = 384
 EPS = 1e-05
 NEG = -1e30
 F32 = jnp.float32
@@ -42,6 +43,20 @@
 
 def kernel(
     n,
+    xbc_hbm,
+    gate_hbm,
+    dt_hbm,
+    bias_hbm,
+    alog_hbm,
+    convw_hbm,
+    convb_hbm,
+    skip_hbm,
+    gain_hbm,
+    queries_hbm,
+    keys_hbm,
+    values_hbm,
+    mamba_out,
+    attn_out,
     xbc,
     gate,
     dt_raw,
@@ -54,20 +69,26 @@
     queries,
     keys,
     values,
-    mamba_out,
-    attn_out,
-    rim,
+    rim_wide,
+    rim_tall,
+    rim_src,
+    rim_dst,
     xc,
     kbuf,
     vbuf,
     dt_row,
     cum_row,
+    skip_row,
     ecum_x,
     spread,
     s_own,
     h_in,
     h_out,
+    r_in,
+    r_out,
+    c_next,
     y_acc,
+    in_sems,
     rim_send,
     rim_recv,
     k_send,
@@ -76,6 +97,10 @@
     v_recv,
     h_send,
     h_recv,
+    r_send,
+    r_recv,
+    c_send,
+    c_recv,
 ):
     me = lax.axis_index("ctx")
     rows = xbc.shape[0]
@@ -92,14 +117,35 @@
     has_next = me < n - 1
     has_prev = me > 0
     right = me + 1
-
-    def remote(src, dst, send, recv):
+    is_last = me == n - 1
+    before_last = me == n - 2
+    pieces_wide = xbc.shape[1] // RIM_WIDTH
+
+    pairs = (
+        (xbc_hbm, xbc),
+        (dt_hbm, dt_raw),
+        (bias_hbm, dt_bias),
+        (alog_hbm, a_log),
+        (convw_hbm, conv_w),
+        (convb_hbm, conv_b),
+        (skip_hbm, skip),
+        (keys_hbm, keys),
+        (values_hbm, values),
+        (queries_hbm, queries),
+        (gate_hbm, gate),
+        (gain_hbm, gain),
+    )
+    loads = [pltpu.make_async_copy(a, b, in_sems.at[i]) for i, (a, b) in enumerate(pairs)]
+    for load in loads:
+        load.start()
+
+    def remote(src, dst, send, recv, to):
         return pltpu.make_async_remote_copy(
             src_ref=src,
             dst_ref=dst,
             send_sem=send,
             recv_sem=recv,
-            device_id={"ctx": right},
+            device_id={"ctx": to},
             device_id_type=pl.DeviceIdType.MESH,
         )
 
@@ -111,37 +157,60 @@
             barrier, inc=1, device_id={"ctx": me - 1}, device_id_type=pl.DeviceIdType.MESH
         )
 
-    @pl.when(has_next)
-    def _():
-        pl.semaphore_wait(barrier, 1)
+    @pl.when(before_last)
+    def _():
+        pl.semaphore_signal(
+            barrier, inc=1, device_id={"ctx": me + 1}, device_id_type=pl.DeviceIdType.MESH
+        )
 
     def rim_copy():
-        return remote(xbc.at[pl.ds(rows - RIM, RIM), :], rim, rim_send, rim_recv)
+        return remote(rim_src, rim_dst, rim_send, rim_recv, right)
 
     def own_kv():
         return (
-            remote(keys, kbuf.at[me], k_send.at[me], k_recv.at[me]),
-            remote(values, vbuf.at[me], v_send.at[me], v_recv.at[me]),
+            remote(keys_hbm, kbuf.at[me], k_send.at[me], k_recv.at[me], right),
+            remote(values_hbm, vbuf.at[me], v_send.at[me], v_recv.at[me], right),
         )
 
     def kv_copy(block):
         return (
-            remote(kbuf.at[block], kbuf.at[block], k_send.at[block], k_recv.at[block]),
-            remote(vbuf.at[block], vbuf.at[block], v_send.at[block], v_recv.at[block]),
+            remote(kbuf.at[block], kbuf.at[block], k_send.at[block], k_recv.at[block], right),
+            remote(vbuf.at[block], vbuf.at[block], v_send.at[block], v_recv.at[block], right),
         )
 
     def h_copy(c):
-        return remote(h_out.at[c], h_in.at[c], h_send.at[c], h_recv.at[c])
+        return remote(h_out.at[c], h_in.at[c], h_send.at[c], h_recv.at[c], right)
+
+    def r_copy(c):
+        return remote(r_out.at[c], r_in.at[c], r_send.at[c], r_recv.at[c], right)
+
+    def c_copy():
+        return remote(
+            xc.at[:, pl.ds(head_cols + groups * N_STATE, groups * N_STATE)],
+            c_next,
+            c_send,
+            c_recv,
+            me - 1,
+        )
+
+    @pl.when(has_next | is_last)
+    def _():
+        pl.semaphore_wait(barrier, 1)
+
+    loads[0].wait()
 
     @pl.when(has_next)
     def _():
+        last = xbc[rows - RIM :, :].astype(F32)
+        for p in range(pieces_wide):
+            rim_tall[p * 3 : p * 3 + 3, :] = last[
+                RIM - 3 :, p * RIM_WIDTH : (p + 1) * RIM_WIDTH
+            ]
+        rim_src[...] = rim_tall[...].astype(BF16)
         rim_copy().start()
         for copy in own_kv():
             copy.start()
 
-    kbuf[me] = keys[...]
-    vbuf[me] = values[...]
-
     def clear(j, carry):
         @pl.when(j > me)
         def _():
@@ -151,6 +220,8 @@
         return carry
 
     lax.fori_loop(0, n, clear, 0)
+    for load in loads[1:7]:
+        load.wait()
 
     def column(ref):
         return jnp.transpose(jnp.broadcast_to(ref[...], (rows, heads)))
@@ -163,6 +234,7 @@
     while step < rows:
         cum = cum + jnp.where(lane >= step, pltpu.roll(cum, step, 1), 0.0)
         step *= 2
+    skip_row[...] = column(skip)
     dt_row[...] = dt
     cum_row[...] = cum
     spread_row = lax.broadcasted_iota(jnp.int32, (3 * per_group, gcols), 0)
@@ -178,25 +250,39 @@
         parts = jnp.transpose(jnp.concatenate([hi, mid, low], axis=0))
         return dot(parts.astype(BF16), spread[...])
 
+    rim_wide[...] = jnp.zeros(rim_wide.shape, F32)
+
     @pl.when(has_prev)
     def _():
         rim_copy().wait_recv()
-
-    @pl.when(me == 0)
-    def _():
-        rim[...] = jnp.zeros(rim.shape, BF16)
+        rim_tall[...] = rim_dst[...].astype(F32)
+        for p in range(pieces_wide):
+            rim_wide[5:, p * RIM_WIDTH : (p + 1) * RIM_WIDTH] = rim_tall[p * 3 : p * 3 + 3, :]
 
     def conv_tile(start, width):
         cols = pl.ds(pl.multiple_of(start, 256), width)
-        ext = jnp.concatenate([rim[:, cols].astype(F32), xbc[:, cols].astype(F32)], axis=0)
+        ext = jnp.concatenate([rim_wide[:, cols], xbc[:, cols].astype(F32)], axis=0)
         acc = jnp.broadcast_to(conv_b[:, cols], (rows, width))
         for tap in range(taps):
             by = taps - 1 - tap
             moved = ext if by == 0 else pltpu.roll(ext, by, 0)
-            acc = acc + conv_w[tap : tap + 1, cols] * moved[RIM:]
+            acc = acc + conv_w[tap : tap + 1, cols] * moved[8:]
         out = silu(acc)
         xc[:, cols] = out.astype(BF16)
         return out
+
+    def relay(s):
+        block = me - 1 - s
+
+        @pl.when(block >= 0)
+        def _():
+            for copy in kv_copy(block):
+                copy.wait_recv()
+
+            @pl.when(has_next)
+            def _():
+                for copy in kv_copy(block):
+                    copy.start()
 
     def group_rows(g):
         return pl.ds(pl.multiple_of(g * per_group, per_group), per_group)
@@ -222,9 +308,23 @@
 
         ecum_x[:, pl.ds(pl.multiple_of(g * gcols, gcols), gcols)] = expand(jnp.exp(cum_g))
         conv_tile(head_cols + (groups + g) * N_STATE, N_STATE)
+
+        @pl.when(g == max(groups - 2, 0))
+        def _():
+            relay(0)
+
         return carry
 
     lax.fori_loop(0, groups, first, 0)
+
+    @pl.when(is_last)
+    def _():
+        c_copy().start()
+
+    for load in loads[7:]:
+        load.wait()
+    kbuf[me] = keys[...]
+    vbuf[me] = values[...]
 
     def within(g):
         b_part = xc[:, pl.ds(pl.multiple_of(head_cols + g * N_STATE, N_STATE), N_STATE)]
@@ -232,6 +332,7 @@
         products = dot_nt(c_part, b_part)
         cum_g = cum_row[group_rows(g), :]
         dt_g = dt_row[group_rows(g), :]
+        skip_g = skip_row[group_rows(g), :]
         cum_t = jnp.transpose(cum_g)
         t_pos = lax.broadcasted_iota(jnp.int32, (rows, rows), 0)
         s_pos = lax.broadcasted_iota(jnp.int32, (rows, rows), 1)
@@ -249,7 +350,7 @@
                 [jnp.where(low_half, x_pair, 0.0), jnp.where(low_half, 0.0, x_pair)], axis=0
             ).astype(BF16)
             scale = jnp.where(
-                low_half, skip[g * per_group + 2 * pair], skip[g * per_group + 2 * pair + 1]
+                low_half[:1], skip_g[2 * pair : 2 * pair + 1], skip_g[2 * pair + 1 : 2 * pair + 2]
             )
             y_acc[:, cols] = dot(jnp.concatenate(mixes, axis=1), x_two) + scale * x_pair
 
@@ -273,19 +374,6 @@
             total = jnp.sum(probs, axis=1, keepdims=True)
             attn_out[:, cols] = (dot(probs.astype(BF16), v_all) / total).astype(BF16)
 
-    def relay(s):
-        block = me - 1 - s
-
-        @pl.when(block >= 0)
-        def _():
-            for copy in kv_copy(block):
-                copy.wait_recv()
-
-            @pl.when(has_next)
-            def _():
-                for copy in kv_copy(block):
-                    copy.start()
-
     def finish(g):
         cols = pl.ds(pl.multiple_of(g * gcols, gcols), gcols)
         v = y_acc[:, cols] * silu(gate[:, cols].astype(F32))
@@ -295,31 +383,47 @@
     def chain(c, carry):
         g = c // per_chunks
         cols = pl.ds(pl.multiple_of(c * CHUNK, CHUNK), CHUNK)
-
-        @pl.when(c < n - 1)
+        c_cols = pl.ds(pl.multiple_of(head_cols + (groups + g) * N_STATE, N_STATE), N_STATE)
+        n_cols = pl.ds(pl.multiple_of(g * N_STATE, N_STATE), N_STATE)
+
+        @pl.when((c >= 1) & (c < n - 1))
         def _():
             relay(c)
 
-        @pl.when(has_prev)
+        def passed():
+            total = ecum_x[rows - 1 : rows, cols]
+            return (total * h_in[c].astype(F32) + s_own[c]).astype(BF16)
+
+        @pl.when(has_prev & has_next)
         def _():
             h_copy(c).wait_recv()
 
-            @pl.when(has_next)
+        @pl.when(has_prev & (me < n - 2))
+        def _():
+            h_out[c] = passed()
+            h_copy(c).start()
+
+        @pl.when(before_last)
+        def _():
+            @pl.when(c == 0)
             def _():
-                total = ecum_x[rows - 1 : rows, cols]
-                h_out[c] = (total * h_in[c].astype(F32) + s_own[c]).astype(BF16)
-                h_copy(c).start()
+                c_copy().wait_recv()
+
+            r_out[c] = dot(c_next[:, n_cols], passed()).astype(BF16)
+            r_copy(c).start()
 
         @pl.when(c < groups)
         def _():
             within(c)
 
-        @pl.when(has_prev)
-        def _():
-            c_cols = pl.ds(
-                pl.multiple_of(head_cols + (groups + g) * N_STATE, N_STATE), N_STATE
-            )
+        @pl.when(has_prev & has_next)
+        def _():
             y_acc[:, cols] += ecum_x[:, cols] * dot(xc[:, c_cols], h_in[c])
+
+        @pl.when(is_last)
+        def _():
+            r_copy(c).wait_recv()
+            y_acc[:, cols] += ecum_x[:, cols] * r_in[c].astype(F32)
 
         @pl.when(lax.rem(c, per_chunks) == per_chunks - 1)
         def _():
@@ -335,7 +439,7 @@
 
     lead = max(n - 1, groups)
     lax.fori_loop(0, chunks, chain, 0)
-    for s in range(chunks, n - 1):
+    for s in range(max(chunks, 1), n - 1):
         relay(s)
 
     def rest(piece, carry):
@@ -350,12 +454,6 @@
         rim_copy().wait_send()
         for copy in own_kv():
             copy.wait_send()
-
-        def sent(c, carry):
-            h_copy(c).wait_send()
-            return carry
-
-        lax.fori_loop(0, chunks, sent, 0)
 
         def sent_kv(block, carry):
             @pl.when(block < me)
@@ -366,6 +464,26 @@
             return carry
 
         lax.fori_loop(0, n, sent_kv, 0)
+
+    def sent_h(c, carry):
+        h_copy(c).wait_send()
+        return carry
+
+    def sent_r(c, carry):
+        r_copy(c).wait_send()
+        return carry
+
+    @pl.when(me < n - 2)
+    def _():
+        lax.fori_loop(0, chunks, sent_h, 0)
+
+    @pl.when(before_last)
+    def _():
+        lax.fori_loop(0, chunks, sent_r, 0)
+
+    @pl.when(is_last)
+    def _():
+        c_copy().wait_send()
 
 
 def shards(
@@ -390,21 +508,41 @@
     per_group = heads // groups
     chunks = head_cols // CHUNK
     vmem = pl.BlockSpec(memory_space=pltpu.VMEM)
-    smem = pl.BlockSpec(memory_space=pltpu.SMEM)
+    hbm = pl.BlockSpec(memory_space=pltpu.HBM)
     dma = pltpu.SemaphoreType.DMA
+    args = (
+        xbc,
+        gate_in,
+        dt_raw,
+        dt_bias.reshape(1, -1),
+        a_log.reshape(1, -1),
+        conv_weight,
+        conv_bias.reshape(1, -1),
+        skip_weight.reshape(1, -1),
+        norm_gain.reshape(1, -1),
+        queries,
+        keys,
+        values,
+    )
+    rim_rows = -(-(3 * (xbc.shape[1] // RIM_WIDTH)) // RIM) * RIM
     return pl.pallas_call(
         functools.partial(kernel, n),
         out_shape=(
             jax.ShapeDtypeStruct((rows, head_cols), BF16),
             jax.ShapeDtypeStruct(queries.shape, BF16),
         ),
-        in_specs=[vmem] * 7 + [smem] + [vmem] * 4,
+        in_specs=[hbm] * len(args),
         out_specs=(vmem, vmem),
-        scratch_shapes=[
-            pltpu.VMEM((RIM, xbc.shape[1]), BF16),
+        scratch_shapes=[pltpu.VMEM(a.shape, a.dtype) for a in args]
+        + [
+            pltpu.VMEM((8, xbc.shape[1]), F32),
+            pltpu.VMEM((rim_rows, RIM_WIDTH), F32),
+            pltpu.VMEM((rim_rows, RIM_WIDTH), BF16),
+            pltpu.VMEM((rim_rows, RIM_WIDTH), BF16),
             pltpu.VMEM(xbc.shape, BF16),
             pltpu.VMEM((n,) + keys.shape, BF16),
             pltpu.VMEM((n,) + values.shape, BF16),
+            pltpu.VMEM(dt_raw.shape, F32),
             pltpu.VMEM(dt_raw.shape, F32),
             pltpu.VMEM(dt_raw.shape, F32),
             pltpu.VMEM((rows, head_cols), F32),
@@ -412,7 +550,11 @@
             pltpu.VMEM((chunks, N_STATE, CHUNK), F32),
             pltpu.VMEM((chunks, N_STATE, CHUNK), BF16),
             pltpu.VMEM((chunks, N_STATE, CHUNK), BF16),
+            pltpu.VMEM((chunks, rows, CHUNK), BF16),
+            pltpu.VMEM((chunks, rows, CHUNK), BF16),
+            pltpu.VMEM((rows, groups * N_STATE), BF16),
             pltpu.VMEM((rows, head_cols), F32),
+            dma((len(args),)),
             dma,
             dma,
             dma((n,)),
@@ -421,25 +563,16 @@
             dma((n,)),
             dma((chunks,)),
             dma((chunks,)),
+            dma((chunks,)),
+            dma((chunks,)),
+            dma,
+            dma,
         ],
         compiler_params=pltpu.CompilerParams(
             collective_id=0, has_side_effects=True, vmem_limit_bytes=48 * 1024 * 1024
         ),
         name="mixers",
-    )(
-        xbc,
-        gate_in,
-        dt_raw,
-        dt_bias.reshape(1, -1),
-        a_log.reshape(1, -1),
-        conv_weight,
-        conv_bias.reshape(1, -1),
-        skip_weight,
-        norm_gain.reshape(1, -1),
-        queries,
-        keys,
-        values,
-    )
+    )(*args)
 
 
 def solution(mesh):

time: 86.8 us -> 78.6 us (0.906)
  Pallas kernels: 73 us -> 64.8 us
    pallas_call x1, Pallas kernels: 73 us -> 64.8 us  [shards(): pl.pallas_call(functools.partial(kernel, n), out_shape=(jax.ShapeDtypeStr...]
where the time goes in v2:
time: 78.6 us; the launch traced here: 78.1 us
  Pallas kernels  64.8 us (82%)
  local copies, waits for them, and re-layouts  12.7 us (16%)
    pallas_call x1, Pallas kernels, shards(): pl.pallas_call(functools.partial(kernel, n), out_shape=(jax.ShapeDtypeStr...  64.8 us
    unnamed x26, local copies, waits for them, and re-layouts  12.7 us

profile of v2, /device:TPU:24, one launch (start us, length us, event | category | flops | bytes accessed | tf_op | source)
XLA Modules:
  0.0 78.1 jit_solution(9682209209998160052)
XLA Ops:
  0.6 0.0 copy-start
  0.6 1.4 %copy-done = bf16[128,6144]{1,0:T(8,128)(2,1)S(1)} copy-done((bf16[128,6144]{1,0:T(8,128)(2,1)S(1)}, bf16[128,6144]{1,0:T(8,128)(2,1)}, u32[]{:S(2)}) %copy-start) | copy-done | bytes 1572888
  2.0 0.0 copy-start.1
  2.0 1.2 %copy-done.1 = bf16[128,4096]{1,0:T(8,128)(2,1)S(1)} copy-done((bf16[128,4096]{1,0:T(8,128)(2,1)S(1)}, bf16[128,4096]{1,0:T(8,128)(2,1)}, u32[]{:S(2)}) %copy-start.1) | copy-done | bytes 1048600
  3.3 0.0 copy-start.2
  3.3 1.2 %copy-done.2 = bf16[128,4096]{1,0:T(8,128)(2,1)S(1)} copy-done((bf16[128,4096]{1,0:T(8,128)(2,1)S(1)}, bf16[128,4096]{1,0:T(8,128)(2,1)}, u32[]{:S(2)}) %copy-start.2) | copy-done | bytes 1048600
  4.5 0.0 copy-start.3
  4.5 0.9 %copy-done.3 = bf16[128,512]{1,0:T(8,128)(2,1)S(1)} copy-done((bf16[128,512]{1,0:T(8,128)(2,1)S(1)}, bf16[128,512]{1,0:T(8,128)(2,1)}, u32[]{:S(2)}) %copy-start.3) | copy-done | bytes 131096
  5.4 0.0 copy-start.4
  5.4 0.9 %copy-done.4 = bf16[128,512]{1,0:T(8,128)(2,1)S(1)} copy-done((bf16[128,512]{1,0:T(8,128)(2,1)S(1)}, bf16[128,512]{1,0:T(8,128)(2,1)}, u32[]{:S(2)}) %copy-start.4) | copy-done | bytes 131096
  6.3 0.0 copy-start.5
  6.3 0.9 %copy-done.5 = f32[4,6144]{1,0:T(4,128)S(1)} copy-done((f32[4,6144]{1,0:T(4,128)S(1)}, f32[4,6144]{1,0:T(4,128)}, u32[]{:S(2)}) %copy-start.5) | copy-done | bytes 98328
  7.2 0.0 copy-start.6
  7.2 0.8 copy-done.6
  8.0 0.0 copy-start.7
  8.0 0.7 copy-done.7
  8.7 0.0 copy-start.8
  8.7 0.7 copy-done.8
  9.4 0.0 copy-start.9
  9.4 0.7 copy-done.9
  10.1 0.0 copy-start.10
  10.1 0.7 copy-done.10
  10.7 0.0 copy-start.11
  10.7 0.7 copy-done.11
  11.4 64.8 %mixers.1 = (bf16[128,4096]{1,0:T(8,128)(2,1)S(1)}, bf16[128,4096]{1,0:T(8,128)(2,1)S(1)}) custom-call(bf16[128,6144]{1,0:T(8,128)(2,1)S(1)} %copy-done, bf16[128,4096]{1,0:T(8,128)(2,1)S(1)} %copy-done.1, f32[64,128]{1,0:T(8,128)S(1)} %copy-done.6, f32[1,64]{1,0:T(1,128)S(1)} %bitcast.7, f32[1,64]{1,0:T(1,128)S(1)} %bitcast.8, f32[4,6144]{1,0:T(4,128)S(1)} %copy-done.5, ...), custom_call_target="tpu_custom_call" | custom-call | tf_op jit(solution)/shard_map/mixers/pallas_call | solution.py:528
  76.2 1.0 %copy.16 = bf16[128,4096]{1,0:T(8,128)(2,1)} copy(bf16[128,4096]{1,0:T(8,128)(2,1)S(1)} %get-tuple-element.4) | data formatting | bytes 2097152
  77.1 1.0 %copy.17 = bf16[128,4096]{1,0:T(8,128)(2,1)} copy(bf16[128,4096]{1,0:T(8,128)(2,1)S(1)} %get-tuple-element.5) | data formatting | bytes 2097152
Async XLA Ops:
  0.6 1.4 %copy-start = (bf16[128,6144]{1,0:T(8,128)(2,1)S(1)}, bf16[128,6144]{1,0:T(8,128)(2,1)}, u32[]{:S(2)}) copy-start(bf16[128,6144]{1,0:T(8,128)(2,1)} %xbc_hbm.1) | copy-start | bytes 4718596
  2.0 1.2 %copy-start.1 = (bf16[128,4096]{1,0:T(8,128)(2,1)S(1)}, bf16[128,4096]{1,0:T(8,128)(2,1)}, u32[]{:S(2)}) copy-start(bf16[128,4096]{1,0:T(8,128)(2,1)} %gate_hbm.1) | copy-start | bytes 3145732
  3.3 1.2 %copy-start.2 = (bf16[128,4096]{1,0:T(8,128)(2,1)S(1)}, bf16[128,4096]{1,0:T(8,128)(2,1)}, u32[]{:S(2)}) copy-start(bf16[128,4096]{1,0:T(8,128)(2,1)} %queries_hbm.1) | copy-start | bytes 3145732
  4.5 0.9 %copy-start.3 = (bf16[128,512]{1,0:T(8,128)(2,1)S(1)}, bf16[128,512]{1,0:T(8,128)(2,1)}, u32[]{:S(2)}) copy-start(bf16[128,512]{1,0:T(8,128)(2,1)} %keys_hbm.1) | copy-start | bytes 393220
  5.4 0.9 %copy-start.4 = (bf16[128,512]{1,0:T(8,128)(2,1)S(1)}, bf16[128,512]{1,0:T(8,128)(2,1)}, u32[]{:S(2)}) copy-start(bf16[128,512]{1,0:T(8,128)(2,1)} %values_hbm.1) | copy-start | bytes 393220
  6.3 0.9 %copy-start.5 = (f32[4,6144]{1,0:T(4,128)S(1)}, f32[4,6144]{1,0:T(4,128)}, u32[]{:S(2)}) copy-start(f32[4,6144]{1,0:T(4,128)} %convw_hbm.1) | copy-start | bytes 294916
  7.2 0.8 copy-start.6
  8.0 0.7 copy-start.7
  8.7 0.7 copy-start.8
  9.4 0.7 copy-start.9
  10.1 0.7 copy-start.10
  10.7 0.7 copy-start.11

commit v3 on v2

--- a/solution.py
+++ b/solution.py
@@ -55,6 +55,8 @@
     queries_hbm,
     keys_hbm,
     values_hbm,
+    mamba_hbm,
+    attn_hbm,
     mamba_out,
     attn_out,
     xbc,
@@ -89,6 +91,8 @@
     c_next,
     y_acc,
     in_sems,
+    mamba_sems,
+    attn_sems,
     rim_send,
     rim_recv,
     k_send,
@@ -157,10 +161,16 @@
             barrier, inc=1, device_id={"ctx": me - 1}, device_id_type=pl.DeviceIdType.MESH
         )
 
-    @pl.when(before_last)
+    @pl.when((me >= 2) & has_next)
     def _():
         pl.semaphore_signal(
             barrier, inc=1, device_id={"ctx": me + 1}, device_id_type=pl.DeviceIdType.MESH
+        )
+
+    @pl.when(is_last)
+    def _():
+        pl.semaphore_signal(
+            barrier, inc=1, device_id={"ctx": 0}, device_id_type=pl.DeviceIdType.MESH
         )
 
     def rim_copy():
@@ -176,6 +186,18 @@
         return (
             remote(kbuf.at[block], kbuf.at[block], k_send.at[block], k_recv.at[block], right),
             remote(vbuf.at[block], vbuf.at[block], v_send.at[block], v_recv.at[block], right),
+        )
+
+    def far_kv():
+        return (
+            remote(keys_hbm, kbuf.at[0], k_send.at[n], k_recv.at[0], n - 1),
+            remote(values_hbm, vbuf.at[0], v_send.at[n], v_recv.at[0], n - 1),
+        )
+
+    def back_kv():
+        return (
+            remote(kbuf.at[0], kbuf.at[0], k_send.at[0], k_recv.at[0], me - 1),
+            remote(vbuf.at[0], vbuf.at[0], v_send.at[0], v_recv.at[0], me - 1),
         )
 
     def h_copy(c):
@@ -193,7 +215,11 @@
             me - 1,
         )
 
-    @pl.when(has_next | is_last)
+    @pl.when((me == 0) | ((me >= 3) & has_next))
+    def _():
+        pl.semaphore_wait(barrier, 2)
+
+    @pl.when((me == 1) | (me == 2) | is_last)
     def _():
         pl.semaphore_wait(barrier, 1)
 
@@ -210,6 +236,11 @@
         rim_copy().start()
         for copy in own_kv():
             copy.start()
+
+        @pl.when(me == 0)
+        def _():
+            for copy in far_kv():
+                copy.start()
 
     def clear(j, carry):
         @pl.when(j > me)
@@ -274,12 +305,12 @@
     def relay(s):
         block = me - 1 - s
 
-        @pl.when(block >= 0)
+        @pl.when((block >= 1) | ((block == 0) & (me == 1)))
         def _():
             for copy in kv_copy(block):
                 copy.wait_recv()
 
-            @pl.when(has_next)
+            @pl.when(has_next & (block >= 1))
             def _():
                 for copy in kv_copy(block):
                     copy.start()
@@ -320,6 +351,19 @@
     @pl.when(is_last)
     def _():
         c_copy().start()
+
+    @pl.when(me >= 3)
+    def _():
+        for copy in back_kv():
+            copy.wait_recv()
+        for copy in back_kv():
+            copy.start()
+
+    def wait_third():
+        @pl.when(me == 2)
+        def _():
+            for copy in back_kv():
+                copy.wait_recv()
 
     for load in loads[7:]:
         load.wait()
@@ -358,6 +402,13 @@
     piece_heads = repeat // 2
     log2_scale = 1.4426950408889634 / math.sqrt(KEY_DIM)
 
+    def attn_flush(piece):
+        width = piece_heads * KEY_DIM
+        cols = pl.ds(pl.multiple_of(piece * width, width), width)
+        return pltpu.make_async_copy(
+            attn_out.at[:, cols], attn_hbm.at[:, cols], attn_sems.at[piece]
+        )
+
     def attend(piece):
         kv_cols = pl.ds(pl.multiple_of((piece // 2) * KEY_DIM, KEY_DIM), KEY_DIM)
         k_all = jnp.concatenate([kbuf[j, :, kv_cols] for j in range(n)], axis=0)
@@ -373,12 +424,20 @@
             probs = jnp.exp2((scores - top) * log2_scale)
             total = jnp.sum(probs, axis=1, keepdims=True)
             attn_out[:, cols] = (dot(probs.astype(BF16), v_all) / total).astype(BF16)
+        attn_flush(piece).start()
+
+    def mamba_flush(g):
+        cols = pl.ds(pl.multiple_of(g * gcols, gcols), gcols)
+        return pltpu.make_async_copy(
+            mamba_out.at[:, cols], mamba_hbm.at[:, cols], mamba_sems.at[g]
+        )
 
     def finish(g):
         cols = pl.ds(pl.multiple_of(g * gcols, gcols), gcols)
         v = y_acc[:, cols] * silu(gate[:, cols].astype(F32))
         scale = lax.rsqrt(jnp.mean(v * v, axis=1, keepdims=True) + EPS)
         mamba_out[:, cols] = (v * scale * gain[:, cols]).astype(BF16)
+        mamba_flush(g).start()
 
     def chain(c, carry):
         g = c // per_chunks
@@ -429,6 +488,10 @@
         def _():
             finish(g)
 
+        @pl.when(c == lead)
+        def _():
+            wait_third()
+
         piece = c - lead
 
         @pl.when((piece >= 0) & (piece < pieces))
@@ -446,6 +509,8 @@
         attend(piece)
         return carry
 
+    if chunks <= lead:
+        wait_third()
     if chunks - lead < pieces:
         lax.fori_loop(max(chunks - lead, 0), pieces, rest, 0)
 
@@ -456,7 +521,7 @@
             copy.wait_send()
 
         def sent_kv(block, carry):
-            @pl.when(block < me)
+            @pl.when((block >= 1) & (block < me))
             def _():
                 for copy in kv_copy(block):
                     copy.wait_send()
@@ -484,6 +549,27 @@
     @pl.when(is_last)
     def _():
         c_copy().wait_send()
+
+    @pl.when(me >= 3)
+    def _():
+        for copy in back_kv():
+            copy.wait_send()
+
+    @pl.when(me == 0)
+    def _():
+        for copy in far_kv():
+            copy.wait_send()
+
+    def out_done(g, carry):
+        mamba_flush(g).wait()
+        return carry
+
+    def attn_done(piece, carry):
+        attn_flush(piece).wait()
+        return carry
+
+    lax.fori_loop(0, pieces, attn_done, 0)
+    lax.fori_loop(0, groups, out_done, 0)
 
 
 def shards(
@@ -507,7 +593,6 @@
     groups = (xbc.shape[1] - head_cols) // (2 * N_STATE)
     per_group = heads // groups
     chunks = head_cols // CHUNK
-    vmem = pl.BlockSpec(memory_space=pltpu.VMEM)
     hbm = pl.BlockSpec(memory_space=pltpu.HBM)
     dma = pltpu.SemaphoreType.DMA
     args = (
@@ -532,8 +617,12 @@
             jax.ShapeDtypeStruct(queries.shape, BF16),
         ),
         in_specs=[hbm] * len(args),
-        out_specs=(vmem, vmem),
-        scratch_shapes=[pltpu.VMEM(a.shape, a.dtype) for a in args]
+        out_specs=(hbm, hbm),
+        scratch_shapes=[
+            pltpu.VMEM((rows, head_cols), BF16),
+            pltpu.VMEM(queries.shape, BF16),
+        ]
+        + [pltpu.VMEM(a.shape, a.dtype) for a in args]
         + [
             pltpu.VMEM((8, xbc.shape[1]), F32),
             pltpu.VMEM((rim_rows, RIM_WIDTH), F32),
@@ -555,11 +644,13 @@
             pltpu.VMEM((rows, groups * N_STATE), BF16),
             pltpu.VMEM((rows, head_cols), F32),
             dma((len(args),)),
+            dma((groups,)),
+            dma((2 * keys.shape[1] // KEY_DIM,)),
             dma,
             dma,
+            dma((n + 1,)),
             dma((n,)),
-            dma((n,)),
-            dma((n,)),
+            dma((n + 1,)),
             dma((n,)),
             dma((chunks,)),
             dma((chunks,)),
@@ -569,7 +660,7 @@
             dma,
         ],
         compiler_params=pltpu.CompilerParams(
-            collective_id=0, has_side_effects=True, vmem_limit_bytes=48 * 1024 * 1024
+            collective_id=0, has_side_effects=True, vmem_limit_bytes=63 * 1024 * 1024
         ),
         name="mixers",
     )(*args)

time: 78.6 us -> 75 us (0.954)
  local copies, waits for them, and re-layouts: 12.7 us -> 3.35 us
  Pallas kernels: 64.8 us -> 70.9 us
    unnamed x26 -> x4, local copies, waits for them, and re-layouts: 12.7 us -> 3.35 us
    pallas_call x1, Pallas kernels: 64.8 us -> 70.9 us  [shards(): pl.pallas_call(functools.partial(kernel, n), out_shape=(jax.ShapeDtypeStr...]
where the time goes in v3:
time: 75 us; the launch traced here: 74.9 us
  Pallas kernels  70.9 us (95%)
  local copies, waits for them, and re-layouts  3.35 us (4%)
    pallas_call x1, Pallas kernels, shards(): pl.pallas_call(functools.partial(kernel, n), out_shape=(jax.ShapeDtypeStr...  70.9 us
    unnamed x4, local copies, waits for them, and re-layouts  3.35 us

profile of v3, /device:TPU:24, one launch (start us, length us, event | category | flops | bytes accessed | tf_op | source)
XLA Modules:
  0.0 74.9 jit_solution(11193056054128807389)
XLA Ops:
  0.6 70.9 %mixers.1 = (bf16[128,4096]{1,0:T(8,128)(2,1)}, bf16[128,4096]{1,0:T(8,128)(2,1)}) custom-call(bf16[128,6144]{1,0:T(8,128)(2,1)} %xbc_hbm.1, bf16[128,4096]{1,0:T(8,128)(2,1)} %gate_hbm.1, f32[64,128]{1,0:T(8,128)} %dt_hbm.1, f32[1,64]{1,0:T(1,128)} %bitcast.7, f32[1,64]{1,0:T(1,128)} %bitcast.8, f32[4,6144]{1,0:T(4,128)} %convw_hbm.1, f32[1,6144]{1,0:T(1,128)} %bitcast.5, ...), custom_call_target="tpu_custom_call" | custom-call | tf_op jit(solution)/shard_map/mixers/pallas_call | solution.py:613
  71.5 0.0 copy-start
  71.5 2.4 %copy.16 = bf16[128,4096]{1,0:T(8,128)(2,1)} copy(bf16[128,4096]{1,0:T(8,128)(2,1)} %get-tuple-element.4) | data formatting | bytes 2097152
  73.9 0.0 copy-done
  73.9 1.0 %copy.17 = bf16[128,4096]{1,0:T(8,128)(2,1)} copy(bf16[128,4096]{1,0:T(8,128)(2,1)S(1)} %copy-done) | data formatting | bytes 2097152
Async XLA Ops:
  71.5 2.4 %copy-start = (bf16[128,4096]{1,0:T(8,128)(2,1)S(1)}, bf16[128,4096]{1,0:T(8,128)(2,1)}, u32[]{:S(2)}) copy-start(bf16[128,4096]{1,0:T(8,128)(2,1)} %get-tuple-element.5) | copy-start | bytes 3145732

commit v4 on v2

--- a/solution.py
+++ b/solution.py
@@ -14,6 +14,7 @@
 CHUNK = 256
 RIM = 16
 RIM_WIDTH = 384
+VMEM_BYTES = 63 * 1024 * 1024
 EPS = 1e-05
 NEG = -1e30
 F32 = jnp.float32
@@ -55,6 +56,8 @@
     queries_hbm,
     keys_hbm,
     values_hbm,
+    mamba_hbm,
+    attn_hbm,
     mamba_out,
     attn_out,
     xbc,
@@ -69,6 +72,7 @@
     queries,
     keys,
     values,
+    xbc_last,
     rim_wide,
     rim_tall,
     rim_src,
@@ -89,6 +93,8 @@
     c_next,
     y_acc,
     in_sems,
+    mamba_sems,
+    attn_sems,
     rim_send,
     rim_recv,
     k_send,
@@ -122,6 +128,7 @@
     pieces_wide = xbc.shape[1] // RIM_WIDTH
 
     pairs = (
+        (xbc_hbm.at[pl.ds(rows - RIM, RIM), :], xbc_last),
         (xbc_hbm, xbc),
         (dt_hbm, dt_raw),
         (bias_hbm, dt_bias),
@@ -166,17 +173,17 @@
     def rim_copy():
         return remote(rim_src, rim_dst, rim_send, rim_recv, right)
 
-    def own_kv():
-        return (
-            remote(keys_hbm, kbuf.at[me], k_send.at[me], k_recv.at[me], right),
-            remote(values_hbm, vbuf.at[me], v_send.at[me], v_recv.at[me], right),
-        )
-
-    def kv_copy(block):
-        return (
-            remote(kbuf.at[block], kbuf.at[block], k_send.at[block], k_recv.at[block], right),
-            remote(vbuf.at[block], vbuf.at[block], v_send.at[block], v_recv.at[block], right),
-        )
+    def own_k():
+        return remote(keys_hbm, kbuf.at[me], k_send.at[me], k_recv.at[me], right)
+
+    def own_v():
+        return remote(values_hbm, vbuf.at[me], v_send.at[me], v_recv.at[me], right)
+
+    def k_copy(block):
+        return remote(kbuf.at[block], kbuf.at[block], k_send.at[block], k_recv.at[block], right)
+
+    def v_copy(block):
+        return remote(vbuf.at[block], vbuf.at[block], v_send.at[block], v_recv.at[block], right)
 
     def h_copy(c):
         return remote(h_out.at[c], h_in.at[c], h_send.at[c], h_recv.at[c], right)
@@ -193,23 +200,23 @@
             me - 1,
         )
 
-    @pl.when(has_next | is_last)
-    def _():
-        pl.semaphore_wait(barrier, 1)
-
+    pl.semaphore_wait(barrier, 1)
     loads[0].wait()
 
     @pl.when(has_next)
     def _():
-        last = xbc[rows - RIM :, :].astype(F32)
+        last = xbc_last[...].astype(F32)
         for p in range(pieces_wide):
             rim_tall[p * 3 : p * 3 + 3, :] = last[
                 RIM - 3 :, p * RIM_WIDTH : (p + 1) * RIM_WIDTH
             ]
         rim_src[...] = rim_tall[...].astype(BF16)
         rim_copy().start()
-        for copy in own_kv():
-            copy.start()
+        own_k().start()
+
+        @pl.when(has_prev)
+        def _():
+            own_v().start()
 
     def clear(j, carry):
         @pl.when(j > me)
@@ -220,7 +227,7 @@
         return carry
 
     lax.fori_loop(0, n, clear, 0)
-    for load in loads[1:7]:
+    for load in loads[1:8]:
         load.wait()
 
     def column(ref):
@@ -271,18 +278,31 @@
         xc[:, cols] = out.astype(BF16)
         return out
 
-    def relay(s):
-        block = me - 1 - s
-
-        @pl.when(block >= 0)
-        def _():
-            for copy in kv_copy(block):
-                copy.wait_recv()
+    def passing(copy, block):
+        @pl.when((block >= 0) & (block < me))
+        def _():
+            copy(block).wait_recv()
 
             @pl.when(has_next)
             def _():
-                for copy in kv_copy(block):
-                    copy.start()
+                copy(block).start()
+
+    late = per_chunks
+
+    def relay(c):
+        block = me - 1 - c
+
+        @pl.when(c >= 1)
+        def _():
+            passing(k_copy, block)
+
+            @pl.when(block >= 1)
+            def _():
+                passing(v_copy, block)
+
+        @pl.when((me >= 1) & (c == late + me - 1))
+        def _():
+            passing(v_copy, 0)
 
     def group_rows(g):
         return pl.ds(pl.multiple_of(g * per_group, per_group), per_group)
@@ -309,9 +329,17 @@
         ecum_x[:, pl.ds(pl.multiple_of(g * gcols, gcols), gcols)] = expand(jnp.exp(cum_g))
         conv_tile(head_cols + (groups + g) * N_STATE, N_STATE)
 
-        @pl.when(g == max(groups - 2, 0))
-        def _():
-            relay(0)
+        @pl.when((me == 0) & (g == 0))
+        def _():
+            own_v().start()
+
+        @pl.when(g == min(1, groups - 1))
+        def _():
+            passing(k_copy, me - 1)
+
+        @pl.when((g == groups - 1) & (me >= 2))
+        def _():
+            passing(v_copy, me - 1)
 
         return carry
 
@@ -321,7 +349,7 @@
     def _():
         c_copy().start()
 
-    for load in loads[7:]:
+    for load in loads[8:]:
         load.wait()
     kbuf[me] = keys[...]
     vbuf[me] = values[...]
@@ -358,6 +386,13 @@
     piece_heads = repeat // 2
     log2_scale = 1.4426950408889634 / math.sqrt(KEY_DIM)
 
+    def attn_flush(piece):
+        width = piece_heads * KEY_DIM
+        cols = pl.ds(pl.multiple_of(piece * width, width), width)
+        return pltpu.make_async_copy(
+            attn_out.at[:, cols], attn_hbm.at[:, cols], attn_sems.at[piece]
+        )
+
     def attend(piece):
         kv_cols = pl.ds(pl.multiple_of((piece // 2) * KEY_DIM, KEY_DIM), KEY_DIM)
         k_all = jnp.concatenate([kbuf[j, :, kv_cols] for j in range(n)], axis=0)
@@ -373,12 +408,20 @@
             probs = jnp.exp2((scores - top) * log2_scale)
             total = jnp.sum(probs, axis=1, keepdims=True)
             attn_out[:, cols] = (dot(probs.astype(BF16), v_all) / total).astype(BF16)
+        attn_flush(piece).start()
+
+    def mamba_flush(g):
+        cols = pl.ds(pl.multiple_of(g * gcols, gcols), gcols)
+        return pltpu.make_async_copy(
+            mamba_out.at[:, cols], mamba_hbm.at[:, cols], mamba_sems.at[g]
+        )
 
     def finish(g):
         cols = pl.ds(pl.multiple_of(g * gcols, gcols), gcols)
         v = y_acc[:, cols] * silu(gate[:, cols].astype(F32))
         scale = lax.rsqrt(jnp.mean(v * v, axis=1, keepdims=True) + EPS)
         mamba_out[:, cols] = (v * scale * gain[:, cols]).astype(BF16)
+        mamba_flush(g).start()
 
     def chain(c, carry):
         g = c // per_chunks
@@ -386,9 +429,7 @@
         c_cols = pl.ds(pl.multiple_of(head_cols + (groups + g) * N_STATE, N_STATE), N_STATE)
         n_cols = pl.ds(pl.multiple_of(g * N_STATE, N_STATE), N_STATE)
 
-        @pl.when((c >= 1) & (c < n - 1))
-        def _():
-            relay(c)
+        relay(c)
 
         def passed():
             total = ecum_x[rows - 1 : rows, cols]
@@ -437,10 +478,10 @@
 
         return carry
 
-    lead = max(n - 1, groups)
+    lead = max(late + n - 1, groups)
     lax.fori_loop(0, chunks, chain, 0)
-    for s in range(max(chunks, 1), n - 1):
-        relay(s)
+    for c in range(chunks, late + n - 1):
+        relay(c)
 
     def rest(piece, carry):
         attend(piece)
@@ -452,14 +493,14 @@
     @pl.when(has_next)
     def _():
         rim_copy().wait_send()
-        for copy in own_kv():
-            copy.wait_send()
+        own_k().wait_send()
+        own_v().wait_send()
 
         def sent_kv(block, carry):
             @pl.when(block < me)
             def _():
-                for copy in kv_copy(block):
-                    copy.wait_send()
+                k_copy(block).wait_send()
+                v_copy(block).wait_send()
 
             return carry
 
@@ -484,6 +525,32 @@
     @pl.when(is_last)
     def _():
         c_copy().wait_send()
+
+    def out_done(g, carry):
+        mamba_flush(g).wait()
+        return carry
+
+    def attn_done(piece, carry):
+        attn_flush(piece).wait()
+        return carry
+
+    lax.fori_loop(0, pieces, attn_done, 0)
+    lax.fori_loop(0, groups, out_done, 0)
+
+
+def hand_on(mamba_src, attn_src, mamba_dst, attn_dst, sems):
+    half = mamba_src.shape[0] // 2
+    copies = []
+    for i, (src, dst) in enumerate(((mamba_src, mamba_dst), (attn_src, attn_dst))):
+        for j in range(2):
+            part = pl.ds(j * half, half)
+            copies.append(
+                pltpu.make_async_copy(src.at[part, :], dst.at[part, :], sems.at[2 * i + j])
+            )
+    for copy in copies:
+        copy.start()
+    for copy in copies:
+        copy.wait()
 
 
 def shards(
@@ -507,7 +574,6 @@
     groups = (xbc.shape[1] - head_cols) // (2 * N_STATE)
     per_group = heads // groups
     chunks = head_cols // CHUNK
-    vmem = pl.BlockSpec(memory_space=pltpu.VMEM)
     hbm = pl.BlockSpec(memory_space=pltpu.HBM)
     dma = pltpu.SemaphoreType.DMA
     args = (
@@ -525,16 +591,22 @@
         values,
     )
     rim_rows = -(-(3 * (xbc.shape[1] // RIM_WIDTH)) // RIM) * RIM
-    return pl.pallas_call(
+    out_shape = (
+        jax.ShapeDtypeStruct((rows, head_cols), BF16),
+        jax.ShapeDtypeStruct(queries.shape, BF16),
+    )
+    outs = pl.pallas_call(
         functools.partial(kernel, n),
-        out_shape=(
-            jax.ShapeDtypeStruct((rows, head_cols), BF16),
-            jax.ShapeDtypeStruct(queries.shape, BF16),
-        ),
+        out_shape=out_shape,
         in_specs=[hbm] * len(args),
-        out_specs=(vmem, vmem),
-        scratch_shapes=[pltpu.VMEM(a.shape, a.dtype) for a in args]
+        out_specs=(hbm, hbm),
+        scratch_shapes=[
+            pltpu.VMEM((rows, head_cols), BF16),
+            pltpu.VMEM(queries.shape, BF16),
+        ]
+        + [pltpu.VMEM(a.shape, a.dtype) for a in args]
         + [
+            pltpu.VMEM((RIM, xbc.shape[1]), BF16),
             pltpu.VMEM((8, xbc.shape[1]), F32),
             pltpu.VMEM((rim_rows, RIM_WIDTH), F32),
             pltpu.VMEM((rim_rows, RIM_WIDTH), BF16),
@@ -554,7 +626,9 @@
             pltpu.VMEM((chunks, rows, CHUNK), BF16),
             pltpu.VMEM((rows, groups * N_STATE), BF16),
             pltpu.VMEM((rows, head_cols), F32),
-            dma((len(args),)),
+            dma((len(args) + 1,)),
+            dma((groups,)),
+            dma((2 * keys.shape[1] // KEY_DIM,)),
             dma,
             dma,
             dma((n,)),
@@ -569,10 +643,19 @@
             dma,
         ],
         compiler_params=pltpu.CompilerParams(
-            collective_id=0, has_side_effects=True, vmem_limit_bytes=48 * 1024 * 1024
+            collective_id=0, has_side_effects=True, vmem_limit_bytes=VMEM_BYTES
         ),
         name="mixers",
     )(*args)
+    return pl.pallas_call(
+        hand_on,
+        out_shape=out_shape,
+        in_specs=[hbm, hbm],
+        out_specs=(hbm, hbm),
+        scratch_shapes=[dma((4,))],
+        compiler_params=pltpu.CompilerParams(vmem_limit_bytes=VMEM_BYTES),
+        name="hand_on",
+    )(*outs)
 
 
 def solution(mesh):

time: 78.6 us -> 130 us (1.65)
  Pallas kernels: 64.8 us -> 129 us
  local copies, waits for them, and re-layouts: 12.7 us -> 0 us
    pallas_call x1 -> x2, Pallas kernels: 64.8 us -> 129 us  [the longest x1 64.7 us: shards(): pl.pallas_call(hand_on, out_shape=out_shape, in_specs=[hbm, hbm], out_spe...]
    unnamed x26 -> x0, local copies, waits for them, and re-layouts: 12.7 us -> none
where the time goes in v4:
time: 130 us
  Pallas kernels  129 us (99%)
    pallas_call x1, Pallas kernels, shards(): pl.pallas_call(hand_on, out_shape=out_shape, in_specs=[hbm, hbm], out_spe...  64.7 us
    pallas_call x1, Pallas kernels, shards(): pl.pallas_call(functools.partial(kernel, n), out_shape=out_shape, in_spec...  64.5 us

profile of v4, /device:TPU:24, one launch (start us, length us, event | category | flops | bytes accessed | tf_op | source)
XLA Modules:
  0.0 129.8 jit_solution(17756012498127563739)
XLA Ops:
  0.6 64.5 %mixers.1 = (bf16[128,4096]{1,0:T(8,128)(2,1)}, bf16[128,4096]{1,0:T(8,128)(2,1)}) custom-call(bf16[128,6144]{1,0:T(8,128)(2,1)} %xbc_hbm.1, bf16[128,4096]{1,0:T(8,128)(2,1)} %gate_hbm.1, f32[64,128]{1,0:T(8,128)} %dt_hbm.1, f32[1,64]{1,0:T(1,128)} %bitcast.7, f32[1,64]{1,0:T(1,128)} %bitcast.8, f32[4,6144]{1,0:T(4,128)} %convw_hbm.1, f32[1,6144]{1,0:T(1,128)} %bitcast.5, ...), custom_call_target="tpu_custom_call" | custom-call | tf_op jit(solution)/shard_map/mixers/pallas_call | solution.py:598
  65.1 64.7 %hand_on.1 = (bf16[128,4096]{1,0:T(8,128)(2,1)}, bf16[128,4096]{1,0:T(8,128)(2,1)}) custom-call(bf16[128,4096]{1,0:T(8,128)(2,1)} %get-tuple-element.4.mamba_src, bf16[128,4096]{1,0:T(8,128)(2,1)} %get-tuple-element.5.attn_src), custom_call_target="tpu_custom_call" | custom-call | tf_op jit(solution)/shard_map/hand_on/pallas_call | solution.py:650

commit v5 on v4

--- a/solution.py
+++ b/solution.py
@@ -11,7 +11,8 @@
 P_DIM = 64
 N_STATE = 256
 KEY_DIM = 128
-CHUNK = 256
+CHUNK = 128
+TILE = 256
 RIM = 16
 RIM_WIDTH = 384
 VMEM_BYTES = 63 * 1024 * 1024
@@ -314,17 +315,20 @@
         dt_g = dt_row[group_rows(g), :]
         last = jnp.broadcast_to(cum_g[:, rows - 1 :], cum_g.shape)
         tail = expand(dt_g * jnp.exp(last - cum_g))
-        for i in range(per_chunks):
-            c = g * per_chunks + i
-            x_part = conv_tile(c * CHUNK, CHUNK).astype(BF16).astype(F32)
-            weighted = (x_part * tail[:, i * CHUNK : (i + 1) * CHUNK]).astype(BF16)
+        for i in range(gcols // TILE):
+            x_part = conv_tile(g * gcols + i * TILE, TILE).astype(BF16).astype(F32)
+            weighted = (x_part * tail[:, i * TILE : (i + 1) * TILE]).astype(BF16)
             own = dot(b_turned, weighted)
-            s_own[c] = own
+            for j in range(TILE // CHUNK):
+                c = g * per_chunks + i * (TILE // CHUNK) + j
+                s_own[c] = own[:, j * CHUNK : (j + 1) * CHUNK]
 
             @pl.when(me == 0)
             def _():
-                h_out[c] = own.astype(BF16)
-                h_copy(c).start()
+                for j in range(TILE // CHUNK):
+                    c = g * per_chunks + i * (TILE // CHUNK) + j
+                    h_out[c] = own[:, j * CHUNK : (j + 1) * CHUNK].astype(BF16)
+                    h_copy(c).start()
 
         ecum_x[:, pl.ds(pl.multiple_of(g * gcols, gcols), gcols)] = expand(jnp.exp(cum_g))
         conv_tile(head_cols + (groups + g) * N_STATE, N_STATE)
@@ -453,9 +457,9 @@
             r_out[c] = dot(c_next[:, n_cols], passed()).astype(BF16)
             r_copy(c).start()
 
-        @pl.when(c < groups)
-        def _():
-            within(c)
+        @pl.when((lax.rem(c, stride) == 0) & (c < stride * groups))
+        def _():
+            within(c // stride)
 
         @pl.when(has_prev & has_next)
         def _():
@@ -470,15 +474,16 @@
         def _():
             finish(g)
 
-        piece = c - lead
-
-        @pl.when((piece >= 0) & (piece < pieces))
-        def _():
-            attend(piece)
-
-        return carry
-
-    lead = max(late + n - 1, groups)
+        ahead = c - lead
+
+        @pl.when((ahead >= 0) & (ahead < stride * pieces) & (lax.rem(ahead, stride) == 0))
+        def _():
+            attend(ahead // stride)
+
+        return carry
+
+    stride = 2
+    lead = max(late + n - 1, stride * groups)
     lax.fori_loop(0, chunks, chain, 0)
     for c in range(chunks, late + n - 1):
         relay(c)
@@ -487,8 +492,9 @@
         attend(piece)
         return carry
 
-    if chunks - lead < pieces:
-        lax.fori_loop(max(chunks - lead, 0), pieces, rest, 0)
+    done = max(-(-(chunks - lead) // stride), 0)
+    if done < pieces:
+        lax.fori_loop(done, pieces, rest, 0)
 
     @pl.when(has_next)
     def _():
@@ -538,19 +544,28 @@
     lax.fori_loop(0, groups, out_done, 0)
 
 
-def hand_on(mamba_src, attn_src, mamba_dst, attn_dst, sems):
-    half = mamba_src.shape[0] // 2
-    copies = []
-    for i, (src, dst) in enumerate(((mamba_src, mamba_dst), (attn_src, attn_dst))):
-        for j in range(2):
-            part = pl.ds(j * half, half)
-            copies.append(
-                pltpu.make_async_copy(src.at[part, :], dst.at[part, :], sems.at[2 * i + j])
+def hand_on(mamba_src, attn_src, mamba_dst, attn_dst, mamba_mid, attn_mid, sems):
+    quarter = mamba_src.shape[0] // 4
+    loads, stores = [], []
+    for i, (src, mid, dst) in enumerate(
+        ((mamba_src, mamba_mid, mamba_dst), (attn_src, attn_mid, attn_dst))
+    ):
+        for j in range(4):
+            part = pl.ds(j * quarter, quarter)
+            k = 4 * i + j
+            loads.append(
+                pltpu.make_async_copy(src.at[part, :], mid.at[part, :], sems.at[0, k])
             )
-    for copy in copies:
-        copy.start()
-    for copy in copies:
-        copy.wait()
+            stores.append(
+                pltpu.make_async_copy(mid.at[part, :], dst.at[part, :], sems.at[1, k])
+            )
+    for load in loads:
+        load.start()
+    for load, store in zip(loads, stores):
+        load.wait()
+        store.start()
+    for store in stores:
+        store.wait()
 
 
 def shards(
@@ -652,7 +667,7 @@
         out_shape=out_shape,
         in_specs=[hbm, hbm],
         out_specs=(hbm, hbm),
-        scratch_shapes=[dma((4,))],
+        scratch_shapes=[pltpu.VMEM(o.shape, BF16) for o in out_shape] + [dma((2, 8))],
         compiler_params=pltpu.CompilerParams(vmem_limit_bytes=VMEM_BYTES),
         name="hand_on",
     )(*outs)

time: 130 us -> 67.7 us (0.52)
  Pallas kernels: 129 us -> 66.9 us
    pallas_call x1, Pallas kernels: 64.7 us -> 2.4 us  [shards(): pl.pallas_call(hand_on, out_shape=out_shape, in_specs=[hbm, hbm], out_spe...]
where the time goes in v5:
time: 67.7 us; the launch traced here: 67.5 us
  Pallas kernels  66.9 us (99%)
    pallas_call x1, Pallas kernels, shards(): pl.pallas_call(functools.partial(kernel, n), out_shape=out_shape, in_spec...  64.5 us
    pallas_call x1, Pallas kernels, shards(): pl.pallas_call(hand_on, out_shape=out_shape, in_specs=[hbm, hbm], out_spe...  2.4 us

profile of v5, /device:TPU:24, one launch (start us, length us, event | category | flops | bytes accessed | tf_op | source)
XLA Modules:
  0.0 67.5 jit_solution(16148231643571812499)
XLA Ops:
  0.6 64.5 %mixers.1 = (bf16[128,4096]{1,0:T(8,128)(2,1)}, bf16[128,4096]{1,0:T(8,128)(2,1)}) custom-call(bf16[128,6144]{1,0:T(8,128)(2,1)} %xbc_hbm.1, bf16[128,4096]{1,0:T(8,128)(2,1)} %gate_hbm.1, f32[64,128]{1,0:T(8,128)} %dt_hbm.1, f32[1,64]{1,0:T(1,128)} %bitcast.7, f32[1,64]{1,0:T(1,128)} %bitcast.8, f32[4,6144]{1,0:T(4,128)} %convw_hbm.1, f32[1,6144]{1,0:T(1,128)} %bitcast.5, ...), custom_call_target="tpu_custom_call" | custom-call | tf_op jit(solution)/shard_map/mixers/pallas_call | solution.py:613
  65.1 2.4 %hand_on.1 = (bf16[128,4096]{1,0:T(8,128)(2,1)}, bf16[128,4096]{1,0:T(8,128)(2,1)}) custom-call(bf16[128,4096]{1,0:T(8,128)(2,1)} %get-tuple-element.4.mamba_src, bf16[128,4096]{1,0:T(8,128)(2,1)} %get-tuple-element.5.attn_src), custom_call_target="tpu_custom_call" | custom-call | tf_op jit(solution)/shard_map/hand_on/pallas_call | solution.py:665

commit v6 on v5

--- a/solution.py
+++ b/solution.py
@@ -330,7 +330,9 @@
                     h_out[c] = own[:, j * CHUNK : (j + 1) * CHUNK].astype(BF16)
                     h_copy(c).start()
 
-        ecum_x[:, pl.ds(pl.multiple_of(g * gcols, gcols), gcols)] = expand(jnp.exp(cum_g))
+        group_cols = pl.ds(pl.multiple_of(g * gcols, gcols), gcols)
+        ecum_x[:, group_cols] = expand(jnp.exp(cum_g))
+        y_acc[:, group_cols] = jnp.zeros((rows, gcols), F32)
         conv_tile(head_cols + (groups + g) * N_STATE, N_STATE)
 
         @pl.when((me == 0) & (g == 0))
@@ -384,7 +386,7 @@
             scale = jnp.where(
                 low_half[:1], skip_g[2 * pair : 2 * pair + 1], skip_g[2 * pair + 1 : 2 * pair + 2]
             )
-            y_acc[:, cols] = dot(jnp.concatenate(mixes, axis=1), x_two) + scale * x_pair
+            y_acc[:, cols] += dot(jnp.concatenate(mixes, axis=1), x_two) + scale * x_pair
 
     pieces = kv_heads * 2
     piece_heads = repeat // 2
@@ -457,9 +459,11 @@
             r_out[c] = dot(c_next[:, n_cols], passed()).astype(BF16)
             r_copy(c).start()
 
-        @pl.when((lax.rem(c, stride) == 0) & (c < stride * groups))
-        def _():
-            within(c // stride)
+        inner = c - wait_chunks
+
+        @pl.when((inner >= 0) & (inner < stride * groups) & (lax.rem(inner, stride) == 0))
+        def _():
+            within(inner // stride)
 
         @pl.when(has_prev & has_next)
         def _():
@@ -483,7 +487,8 @@
         return carry
 
     stride = 2
-    lead = max(late + n - 1, stride * groups)
+    wait_chunks = min(4, per_chunks - 1)
+    lead = max(late + n - 1, wait_chunks + stride * groups)
     lax.fori_loop(0, chunks, chain, 0)
     for c in range(chunks, late + n - 1):
         relay(c)

time: 67.7 us -> 67.7 us (level)
  no operation moved by 1% of the time
where the time goes in v6:
time: 67.7 us; the launch traced here: 67.5 us
  Pallas kernels  66.9 us (99%)
    pallas_call x1, Pallas kernels, shards(): pl.pallas_call(functools.partial(kernel, n), out_shape=out_shape, in_spec...  64.5 us
    pallas_call x1, Pallas kernels, shards(): pl.pallas_call(hand_on, out_shape=out_shape, in_specs=[hbm, hbm], out_spe...  2.4 us

profile of v6, /device:TPU:24, one launch (start us, length us, event | category | flops | bytes accessed | tf_op | source)
XLA Modules:
  0.0 67.5 jit_solution(10946400282688653772)
XLA Ops:
  0.6 64.5 %mixers.1 = (bf16[128,4096]{1,0:T(8,128)(2,1)}, bf16[128,4096]{1,0:T(8,128)(2,1)}) custom-call(bf16[128,6144]{1,0:T(8,128)(2,1)} %xbc_hbm.1, bf16[128,4096]{1,0:T(8,128)(2,1)} %gate_hbm.1, f32[64,128]{1,0:T(8,128)} %dt_hbm.1, f32[1,64]{1,0:T(1,128)} %bitcast.7, f32[1,64]{1,0:T(1,128)} %bitcast.8, f32[4,6144]{1,0:T(4,128)} %convw_hbm.1, f32[1,6144]{1,0:T(1,128)} %bitcast.5, ...), custom_call_target="tpu_custom_call" | custom-call | tf_op jit(solution)/shard_map/mixers/pallas_call | solution.py:618
  65.1 2.4 %hand_on.1 = (bf16[128,4096]{1,0:T(8,128)(2,1)}, bf16[128,4096]{1,0:T(8,128)(2,1)}) custom-call(bf16[128,4096]{1,0:T(8,128)(2,1)} %get-tuple-element.4.mamba_src, bf16[128,4096]{1,0:T(8,128)(2,1)} %get-tuple-element.5.attn_src), custom_call_target="tpu_custom_call" | custom-call | tf_op jit(solution)/shard_map/hand_on/pallas_call | solution.py:670

commit v7 on v6

--- a/solution.py
+++ b/solution.py
@@ -202,10 +202,14 @@
         )
 
     pl.semaphore_wait(barrier, 1)
-    loads[0].wait()
 
     @pl.when(has_next)
     def _():
+        @pl.when(has_prev)
+        def _():
+            own_k().start()
+
+        loads[0].wait()
         last = xbc_last[...].astype(F32)
         for p in range(pieces_wide):
             rim_tall[p * 3 : p * 3 + 3, :] = last[
@@ -213,11 +217,18 @@
             ]
         rim_src[...] = rim_tall[...].astype(BF16)
         rim_copy().start()
-        own_k().start()
+
+        @pl.when(me == 0)
+        def _():
+            own_k().start()
 
         @pl.when(has_prev)
         def _():
             own_v().start()
+
+    @pl.when(is_last)
+    def _():
+        loads[0].wait()
 
     def clear(j, carry):
         @pl.when(j > me)

time: 67.7 us -> 67.9 us (level)
  no operation moved by 1% of the time
where the time goes in v7:
time: 67.9 us; the launch traced here: 67.7 us
  Pallas kernels  67.1 us (99%)
    pallas_call x1, Pallas kernels, shards(): pl.pallas_call(functools.partial(kernel, n), out_shape=out_shape, in_spec...  64.7 us
    pallas_call x1, Pallas kernels, shards(): pl.pallas_call(hand_on, out_shape=out_shape, in_specs=[hbm, hbm], out_spe...  2.4 us

profile of v7, /device:TPU:24, one launch (start us, length us, event | category | flops | bytes accessed | tf_op | source)
XLA Modules:
  0.0 67.7 jit_solution(6980010490771112638)
XLA Ops:
  0.6 64.7 %mixers.1 = (bf16[128,4096]{1,0:T(8,128)(2,1)}, bf16[128,4096]{1,0:T(8,128)(2,1)}) custom-call(bf16[128,6144]{1,0:T(8,128)(2,1)} %xbc_hbm.1, bf16[128,4096]{1,0:T(8,128)(2,1)} %gate_hbm.1, f32[64,128]{1,0:T(8,128)} %dt_hbm.1, f32[1,64]{1,0:T(1,128)} %bitcast.7, f32[1,64]{1,0:T(1,128)} %bitcast.8, f32[4,6144]{1,0:T(4,128)} %convw_hbm.1, f32[1,6144]{1,0:T(1,128)} %bitcast.5, ...), custom_call_target="tpu_custom_call" | custom-call | tf_op jit(solution)/shard_map/mixers/pallas_call | solution.py:629
  65.3 2.4 %hand_on.1 = (bf16[128,4096]{1,0:T(8,128)(2,1)}, bf16[128,4096]{1,0:T(8,128)(2,1)}) custom-call(bf16[128,4096]{1,0:T(8,128)(2,1)} %get-tuple-element.4.mamba_src, bf16[128,4096]{1,0:T(8,128)(2,1)} %get-tuple-element.5.attn_src), custom_call_target="tpu_custom_call" | custom-call | tf_op jit(solution)/shard_map/hand_on/pallas_call | solution.py:681
